TPU v7x, 768 devices: a whole 4x8x12 slice. The times are simulated.
768 devices in a mesh: dp: 96 (over z, y), tensor: 8 (over x, core).
Axes of the slice: x: 4, y: 8, z: 12, core: 2. Of those that a mesh axis runs over, the one named last changes fastest.
Arguments:
- inputs: bfloat16 [49152, 5120], P('dp', 'tensor'), may hold values from -6 to 6
- cotangent: bfloat16 [49152, 1024], P('dp', 'tensor'), may hold values from -1.5 to 1.5
- base_weight: bfloat16 [5120, 1024], P('tensor'), may hold values from -0.078125 to 0.078125
- down_a: bfloat16 [192, 5120, 16], P('dp', 'tensor'), may hold values from -0.078125 to 0.078125
- up_b: bfloat16 [192, 16, 1024], P('dp', None, 'tensor'), may hold values from -1.5 to 1.5
- block_adapter: int32 [384], P('dp'), may hold values from 0 to 191, as said below
- token_adapter: int32 [49152], P('dp'), may hold values from -1 to 191, as said below
- owner_map: int32 [192], replicated, may hold values from 0 to 191, each once
Outputs:
- gradient_wrt_input: bfloat16 [49152, 5120], P('dp', 'tensor')
- grad_b: float32 [192, 16, 1024], P('dp', None, 'tensor')
Inputs may be any that keep to these rules, and one draw needn't show every extreme that they name: `block_adapter`: each block of 128 rows serves one adapter; some adapters serve many blocks. `token_adapter`: in each block the first rows (at least 32 of them) carry the block's adapter and the rest are padding with -1. A permutation; adapter e stands at slot owner_map[e], on dp index owner_map[e] // 2.
All inputs are finite; a program needn't handle non-finite values.
Results may differ from a plain program's by a relative error of at most 0.0045.
Values may be sent and summed in bfloat16 or wider, within the bound.
No kernel may reach another device: no remote copies, remote signals or barrier semaphores. Data moves between devices by JAX's collectives and lax.ppermute only.
A program may use at most 32 MiB of HBM per device.

v0:
```python
import jax
import jax.numpy as jnp
from jax import lax
from jax.sharding import PartitionSpec as P

adapter_scale_factor = 2.0


def slot_match(slot_ids, row_span, dtype):
    columns = jnp.arange(row_span, dtype=jnp.int32)
    return (slot_ids[:, None] == columns[None, :]).astype(dtype)


def on_device(
    inputs, cotangent, base_weight, down_a, up_b, block_adapter, token_adapter, owner_map
):
    row_count, dpiece = inputs.shape
    kpiece = cotangent.shape[1]
    block_count = block_adapter.shape[0]
    blk_rows = row_count // block_count
    nadapt = owner_map.shape[0]
    own_slots = down_a.shape[0]
    matches = block_adapter[:, None] == jnp.arange(nadapt, dtype=jnp.int32)[None, :]
    slot_ids = jnp.sum(jnp.where(matches, owner_map[None, :], 0), axis=1)
    live_rows = (token_adapter >= 0).astype(jnp.float32)[:, None]
    masked_rows = (cotangent.astype(jnp.float32) * live_rows).astype(jnp.bfloat16)
    input_row_blocks = inputs.reshape(block_count, blk_rows, dpiece)
    g_blocks = masked_rows.reshape(block_count, blk_rows, kpiece)
    shard_piece = lax.all_gather(down_a, "dp", axis=0, tiled=True)
    onehot = slot_match(slot_ids, shard_piece.shape[0], jnp.bfloat16)
    chosen = jnp.einsum("bk,kdr->bdr", onehot, shard_piece, preferred_element_type=jnp.float32)
    selected_down_matrix = chosen.astype(jnp.bfloat16)
    shard_piece = lax.all_gather(up_b, "dp", axis=0, tiled=True)
    onehot = slot_match(slot_ids, shard_piece.shape[0], jnp.bfloat16)
    chosen = jnp.einsum("bk,kro->bro", onehot, shard_piece, preferred_element_type=jnp.float32)
    up_sel = chosen.astype(jnp.bfloat16)
    low_rank_portion = jnp.einsum(
        "aon,anj->aoj", input_row_blocks, selected_down_matrix, preferred_element_type=jnp.float32
    )
    backpart = jnp.einsum("bko,bro->bkr", g_blocks, up_sel, preferred_element_type=jnp.float32)
    low_rank_product, hidden_features = lax.psum((low_rank_portion, backpart), "tensor")
    low_rank_product = (low_rank_product * live_rows.reshape(block_count, blk_rows, 1)).astype(
        jnp.bfloat16
    )
    hidden_features = hidden_features.astype(jnp.bfloat16)
    frozen_path_gradient = lax.dot_general(
        lax.all_gather(masked_rows, "tensor", axis=1, tiled=True),
        base_weight,
        (((1,), (1,)), ((), ())),
        preferred_element_type=jnp.float32,
    )
    adapter_path_gradient = jnp.einsum(
        "eay,exy->eax", hidden_features, selected_down_matrix, preferred_element_type=jnp.float32
    ).reshape(row_count, dpiece)
    gradient_wrt_input = (
        frozen_path_gradient + adapter_scale_factor * adapter_path_gradient
    ).astype(jnp.bfloat16)
    block_partial_terms = adapter_scale_factor * jnp.einsum(
        "bkr,bko->bro", low_rank_product, g_blocks, preferred_element_type=jnp.float32
    )
    onehot = slot_match(slot_ids, lax.axis_size("dp") * own_slots, jnp.float32)
    grad_b = lax.psum_scatter(
        jnp.einsum("bj,bro->jro", onehot, block_partial_terms, precision=lax.Precision.HIGHEST),
        "dp",
        scatter_dimension=0,
        tiled=True,
    )
    return (gradient_wrt_input, grad_b)


def solution(mesh):
    in_specs = (
        P("dp", "tensor"),
        P("dp", "tensor"),
        P("tensor", None),
        P("dp", "tensor", None),
        P("dp", None, "tensor"),
        P("dp"),
        P("dp"),
        P(),
    )
    out_specs = (P("dp", "tensor"), P("dp", None, "tensor"))
    return jax.shard_map(
        on_device, mesh=mesh, in_specs=in_specs, out_specs=out_specs, check_vma=False
    )
```

profile of v0, /device:TPU:2, one launch (start us, length us, event | category | flops | bytes accessed | tf_op | source)
XLA Modules:
  0.0 867.5 jit_solution(11866594513637952217)
XLA Ops:
  7.2 0.0 copy-start
  7.2 0.0 all-gather.5.cloned.1.call-start
  7.2 0.7 all-gather.5.cloned.1.call-update
  7.9 0.0 all-gather.3.cloned.1.call-start
  8.0 0.7 fusion.16
  8.6 1.7 multiply_convert_fusion
  10.3 0.0 copy-start.1
  10.3 0.0 all-gather.3.cloned.1.call-update
  10.4 0.0 reduce-scatter.2.cloned.1.call-start
  10.4 0.9 select_reduce_fusion
  11.3 86.2 %all_gather.10 = bf16[192,16,128]{2,1,0:T(8,128)(2,1)S(1)} all-gather(bf16[2,16,128]{2,1,0:T(8,128)(2,1)} %param.12), channel_id=1, replica_groups=mesh['dp'=96,'tensor'=8] {'dp'}, dimensions={0}, use_global_device_ids=true | all-gather | bytes 794624 | tf_op jit(solution)/shard_map/all_gather | solution.py:33
  97.5 0.3 convolution_convert_fusion
  97.7 0.0 copy-done.1
  97.7 0.2 fusion.11
  97.9 0.0 copy-start.2
  97.9 46.5 %all-gather.5.cloned.1.call-done = bf16[192,640,16]{1,2,0:T(8,128)(2,1)} async-done(((bf16[2,640,16]{1,2,0:T(8,128)(2,1)}), bf16[192,640,16]{1,2,0:T(8,128)(2,1)}) %all-gather.5.cloned.1.call-update) | async-done | bytes 3932176 | tf_op jit(solution)/shard_map/all_gather | solution.py:29
  144.4 3.1 fusion.3
  147.5 0.0 copy-done.2
  147.5 0.3 convolution_bitcast_fusion
  147.8 21.0 %all-reduce = (bf16[4,128,16]{1,2,0:T(8,128)(2,1)S(1)}, f32[4,128,16]{1,2,0:T(8,128)S(1)}) all-reduce(f32[4,128,16]{1,2,0:T(8,128)S(1)} %fusion.11, f32[4,128,16]{1,2,0:T(8,128)S(1)} %convolution_bitcast_fusion), channel_id=1, replica_groups=mesh['dp'=96,'tensor'=8] {'tensor'}, use_global_device_ids=true, to_apply=%region_1.2 | all-reduce | flops 16384 | bytes 114688 | tf_op jit(solution)/shard_map/psum | solution.py:41
  168.8 0.1 convolution_multiply_fusion.1
  169.0 0.9 fusion.9
  170.0 2.1 copy.22
  172.0 0.0 reduce-scatter.2.cloned.1.call-update
  172.1 0.4 convolution_multiply_fusion
  172.4 3.0 all-gather.3.cloned.1.call-done
  175.4 0.0 copy-done
  175.4 3.1 fusion.2
  178.5 682.5 %reduce-scatter.2.cloned.1.call-done = f32[2,16,128]{2,1,0:T(8,128)} async-done(((f32[192,16,128]{2,1,0:T(8,128)}), f32[2,16,128]{2,1,0:T(8,128)}) %reduce-scatter.2.cloned.1.call-update) | async-done | bytes 16400 | tf_op jit(solution)/shard_map/reduce_scatter | solution.py:62
Async XLA Ops:
  7.2 168.3 %copy-start = (bf16[640,1024]{1,0:T(8,128)(2,1)S(1)}, bf16[640,1024]{1,0:T(8,128)(2,1)}, u32[]{:S(2)}) copy-start(bf16[640,1024]{1,0:T(8,128)(2,1)} %param.10) | copy-start | bytes 3932164
  7.2 137.2 %all-gather.5.cloned.1.call-start = ((), (), s32[]{:S(2)}) async-start(), calls=%async_computation.2 | async-start | bytes 3973120 | tf_op jit(solution)/shard_map/all_gather | solution.py:29
  7.9 167.5 %all-gather.3.cloned.1.call-start = ((), (), s32[]{:S(2)}) async-start(), calls=%async_computation.1 | async-start | bytes 1179648 | tf_op jit(solution)/shard_map/all_gather | solution.py:47
  10.3 87.4 %copy-start.1 = (bf16[512,128]{1,0:T(8,128)(2,1)S(1)}, bf16[512,128]{1,0:T(8,128)(2,1)}, u32[]{:S(2)}) copy-start(bf16[512,128]{1,0:T(8,128)(2,1)} %multiply_convert_fusion) | copy-start | bytes 393220
  10.4 850.6 %reduce-scatter.2.cloned.1.call-start = ((), (), s32[]{:S(2)}) async-start(), calls=%async_computation.3 | async-start | bytes 1589248 | tf_op jit(solution)/shard_map/reduce_scatter | solution.py:62
  97.9 49.6 %copy-start.2 = (bf16[512,640]{1,0:T(8,128)(2,1)S(1)}, bf16[512,640]{1,0:T(8,128)(2,1)}, u32[]{:S(2)}) copy-start(bf16[512,640]{1,0:T(8,128)(2,1)} %param.8) | copy-start | bytes 1966084
Sparse Core Ops, SparseCore 0:
  11.8 132.5 all-gather.4
  147.4 28.0 all-gather.2
  181.2 679.7 reduce-scatter.1
where the time goes:
time: 868 us
  waiting for transfers between devices  733 us (84%)
  blocking collectives  107 us (12%)
  between operations  13.8 us (2%)
    reduce_scatter x1, waiting for transfers between devices, on_device(): lax.psum_scatter(jnp.einsum('bj,bro->jro', onehot, block_partial_terms, p...  682 us
    all_gather x1, blocking collectives, on_device(): shard_piece = lax.all_gather(up_b, 'dp', axis=0, tiled=True)  86.2 us
    all_gather x1, waiting for transfers between devices, on_device(): shard_piece = lax.all_gather(down_a, 'dp', axis=0, tiled=True)  46.5 us
    psum x1, blocking collectives, on_device(): lax.psum((low_rank_portion, backpart), 'tensor')  21 us
  transfers between devices with their start and end apart: 3, of which 3 were waited for; matrix products, arithmetic and copies ran while one was open for 2% of the time, Pallas kernels for 0%

commit v1 on v0

v1 whole, which is shorter than its diff:
```python
import jax
import jax.numpy as jnp
from jax import lax
from jax.sharding import PartitionSpec as P

adapter_scale_factor = 2.0
LINE = 8
LANES = 128


def on_device(
    inputs, cotangent, base_weight, down_a, up_b, block_adapter, token_adapter, owner_map
):
    row_count, dpiece = inputs.shape
    kpiece = cotangent.shape[1]
    block_count = block_adapter.shape[0]
    blk_rows = row_count // block_count
    nadapt = owner_map.shape[0]
    own_slots, _, rank = down_a.shape
    dp = lax.axis_size("dp")
    tensor = lax.axis_size("tensor")
    columns = dp // LINE
    chunks = dpiece // LANES
    y_groups = [[z * LINE + y for y in range(LINE)] for z in range(columns)]
    z_groups = [[z * LINE + y for z in range(columns)] for y in range(LINE)]
    my_y = lax.axis_index("dp") % LINE
    my_row = lax.axis_index("dp") // LINE

    full_cotangent = lax.all_gather(cotangent, "tensor", axis=1, tiled=True)

    matches = block_adapter[:, None] == jnp.arange(nadapt, dtype=jnp.int32)[None, :]
    slot_ids = jnp.sum(jnp.where(matches, owner_map[None, :], 0), axis=1)
    live = (token_adapter >= 0).astype(jnp.float32)

    weights = jnp.concatenate([down_a.transpose(0, 2, 1), up_b], axis=2)
    pieces = weights.reshape(own_slots, rank, chunks + 1, LANES).transpose(2, 1, 0, 3)
    pieces = pieces.reshape(dp, own_slots, LANES)
    id_row = jnp.pad(slot_ids, (0, LANES - block_count)).astype(jnp.bfloat16)
    id_rows = jnp.broadcast_to(id_row, (dp, own_slots, LANES))
    table = lax.all_to_all(jnp.concatenate([pieces, id_rows], axis=1), "dp", 0, 0)
    all_slots = table[:, own_slots, :block_count].astype(jnp.int32)
    table = table[:, :own_slots].reshape(dp * own_slots, LANES)

    onehot = (
        all_slots.reshape(-1, 1) == jnp.arange(dp * own_slots, dtype=jnp.int32)[None, :]
    ).astype(jnp.bfloat16)
    picked = jnp.dot(onehot, table, preferred_element_type=jnp.float32).astype(jnp.bfloat16)
    picked = lax.all_to_all(picked.reshape(dp, block_count, LANES), "dp", 0, 0)
    picked = picked.reshape(chunks + 1, rank, block_count, LANES)
    down_sel = picked[:chunks].transpose(2, 1, 0, 3).reshape(block_count, rank, dpiece)
    up_sel = picked[chunks].transpose(1, 0, 2)

    input_blocks = inputs.reshape(block_count, blk_rows, dpiece)
    g_blocks = cotangent.reshape(block_count, blk_rows, kpiece)
    low_part = jnp.einsum("brd,bnd->brn", down_sel, input_blocks, preferred_element_type=jnp.float32)
    hid_part = jnp.einsum("brk,bnk->brn", up_sel, g_blocks, preferred_element_type=jnp.float32)
    part = jnp.concatenate([low_part, hid_part], axis=1).astype(jnp.bfloat16)
    part = lax.all_to_all(jnp.broadcast_to(part, (tensor,) + part.shape), "tensor", 0, 0)
    total = jnp.sum(part.astype(jnp.float32), axis=0) * live.reshape(block_count, 1, blk_rows)
    total = total.astype(jnp.bfloat16)
    low_rank, hidden = total[:, :rank], total[:, rank:]

    terms = adapter_scale_factor * jnp.einsum(
        "brn,bno->bro", low_rank, g_blocks, preferred_element_type=jnp.float32
    )
    terms = terms.astype(jnp.bfloat16)
    terms = lax.all_to_all(
        jnp.broadcast_to(terms, (LINE,) + terms.shape), "dp", 0, 0, axis_index_groups=y_groups
    )
    terms = terms.reshape(LINE * block_count, rank, kpiece)
    row_slots = lax.dynamic_slice_in_dim(all_slots, my_row * LINE, LINE, 0).reshape(-1)
    column_slots = (
        jnp.arange(columns, dtype=jnp.int32)[:, None] * (LINE * own_slots)
        + my_y * own_slots
        + jnp.arange(own_slots, dtype=jnp.int32)[None, :]
    ).reshape(-1)
    owner_match = (column_slots[:, None] == row_slots[None, :]).astype(jnp.bfloat16)
    sums = jnp.einsum("sb,bro->sro", owner_match, terms, preferred_element_type=jnp.float32)
    sums = lax.all_to_all(
        sums.reshape(columns, own_slots, rank, kpiece), "dp", 0, 0, axis_index_groups=z_groups
    )
    grad_b = jnp.sum(sums, axis=0)

    frozen = lax.dot_general(
        full_cotangent, base_weight, (((1,), (1,)), ((), ())), preferred_element_type=jnp.float32
    )
    adapter = jnp.einsum(
        "brn,brd->bnd", hidden, down_sel, preferred_element_type=jnp.float32
    ).reshape(row_count, dpiece)
    gradient = (frozen * live[:, None] + adapter_scale_factor * adapter).astype(jnp.bfloat16)
    return (gradient, grad_b)


def solution(mesh):
    in_specs = (
        P("dp", "tensor"),
        P("dp", "tensor"),
        P("tensor", None),
        P("dp", "tensor", None),
        P("dp", None, "tensor"),
        P("dp"),
        P("dp"),
        P(),
    )
    out_specs = (P("dp", "tensor"), P("dp", None, "tensor"))
    return jax.shard_map(
        on_device, mesh=mesh, in_specs=in_specs, out_specs=out_specs, check_vma=False
    )
```

time: 868 us -> 125 us (0.14)
  waiting for transfers between devices: 733 us -> 44.7 us
  blocking collectives: 107 us -> 36.8 us
  starting transfers between devices: 0.12 us -> 17.7 us
    reduce_scatter x1 -> x0, waiting for transfers between devices: 682 us -> none  [on_device(): lax.psum_scatter(jnp.einsum('bj,bro->jro', onehot, block_partial_terms, p...]
    all_gather x1 -> x0, blocking collectives: 86.2 us -> none  [on_device(): shard_piece = lax.all_gather(up_b, 'dp', axis=0, tiled=True)]
    all_gather x2 -> x1, waiting for transfers between devices: 49.5 us -> 0.01 us  [on_device(): full_cotangent = lax.all_gather(cotangent, 'tensor', axis=1, tiled=True)]
    all_to_all x0 -> x4, waiting for transfers between devices: none -> 44 us  [the longest x1 13.9 us: on_device(): picked = lax.all_to_all(picked.reshape(dp, block_count, LANES), 'dp', 0, 0)]
    all_to_all x0 -> x1, blocking collectives: none -> 36.8 us  [on_device(): lax.all_to_all(jnp.concatenate([pieces, id_rows], axis=1), 'dp', 0, 0)]
    psum x1 -> x0, blocking collectives: 21 us -> none  [on_device(): lax.psum((low_rank_portion, backpart), 'tensor')]
    all_to_all x0 -> x4, starting transfers between devices: none -> 17.7 us  [the longest x1 5.94 us: on_device(): picked = lax.all_to_all(picked.reshape(dp, block_count, LANES), 'dp', 0, 0)]
  transfers between devices with their start and end apart: 3 -> 5, of which waited for: 3 -> 4; matrix products, arithmetic and copies ran while one was open for 2% -> 4% of each run, Pallas kernels for 0% -> 0%
where the time goes in v1:
time: 125 us; the launch traced here: 124 us
  waiting for transfers between devices  44.7 us (36%)
  blocking collectives  36.8 us (29%)
  starting transfers between devices  17.7 us (14%)
  between operations  14.3 us (11%)
  matrix products  5.22 us (4%)
  local copies, waits for them, and re-layouts  2.89 us (2%)
  other arithmetic  2.79 us (2%)
    all_to_all x1, blocking collectives, on_device(): lax.all_to_all(jnp.concatenate([pieces, id_rows], axis=1), 'dp', 0, 0)  36.8 us
    all_to_all x1, waiting for transfers between devices, on_device(): picked = lax.all_to_all(picked.reshape(dp, block_count, LANES), 'dp', 0, 0)  13.9 us
    all_to_all x1, waiting for transfers between devices, on_device(): lax.all_to_all(sums.reshape(columns, own_slots, rank, kpiece), 'dp', 0, 0...  13.5 us
    all_to_all x1, waiting for transfers between devices, on_device(): lax.all_to_all(jnp.broadcast_to(terms, (LINE,) + terms.shape), 'dp', 0, 0...  9.16 us
    all_to_all x1, waiting for transfers between devices, on_device(): lax.all_to_all(jnp.broadcast_to(part, (tensor,) + part.shape), 'tensor',...  7.46 us
    all_to_all x1, starting transfers between devices, on_device(): picked = lax.all_to_all(picked.reshape(dp, block_count, LANES), 'dp', 0, 0)  5.94 us
    all_to_all x1, starting transfers between devices, on_device(): lax.all_to_all(jnp.broadcast_to(part, (tensor,) + part.shape), 'tensor',...  4.84 us
    all_to_all x1, starting transfers between devices, on_device(): lax.all_to_all(sums.reshape(columns, own_slots, rank, kpiece), 'dp', 0, 0...  3.53 us
  transfers between devices with their start and end apart: 5, of which 4 were waited for; matrix products, arithmetic and copies ran while one was open for 4% of the time, Pallas kernels for 0%

profile of v1, /device:TPU:2, one launch (start us, length us, event | category | flops | bytes accessed | tf_op | source)
XLA Modules:
  0.0 124.3 jit_solution(11568959477598890409)
XLA Ops:
  7.2 0.0 copy-start
  7.2 0.0 copy-start.1
  7.2 0.0 copy-start.2
  7.2 1.0 select_reduce_fusion
  8.2 0.8 pad_maximum_fusion.1
  9.0 0.1 reshape.85
  9.2 0.1 copy.31
  9.2 36.8 %all_to_all.25 = bf16[96,4,128]{2,1,0:T(4,128)(2,1)S(1)} all-to-all(bf16[96,4,128]{2,1,0:T(4,128)(2,1)S(1)} %copy.31), channel_id=1, replica_groups=mesh['dp'=96,'tensor'=8] {'dp'}, dimensions={0} | all-to-all | bytes 196608 | tf_op jit(solution)/shard_map/all_to_all | solution.py:40
  46.0 0.2 fusion.12
  46.2 0.1 reshape.93
  46.3 0.9 convolution_convert_fusion
  47.2 5.9 %all-to-all-start.1 = ((bf16[96,4,128]{2,1,0:T(4,128)(2,1)}), bf16[96,4,128]{2,1,0:T(4,128)(2,1)S(1)}, u32[]{:S(2)}, u32[]{:S(2)}) async-start(bf16[96,4,128]{2,1,0:T(4,128)(2,1)} %bitcast.4), calls=%async_computation.1 | async-start | bytes 196608 | tf_op jit(solution)/shard_map/all_to_all | solution.py:48
  53.2 0.0 copy-start.3
  53.2 0.0 all-gather.2.cloned.1.call-start
  53.2 0.7 all-gather.2.cloned.1.call-update
  54.0 13.9 %all-to-all-done.1 = bf16[96,4,128]{2,1,0:T(4,128)(2,1)S(1)} async-done(((bf16[96,4,128]{2,1,0:T(4,128)(2,1)}), bf16[96,4,128]{2,1,0:T(4,128)(2,1)S(1)}, u32[]{:S(2)}, u32[]{:S(2)}) %all-to-all-start.1) | async-done | bytes 98336 | tf_op jit(solution)/shard_map/all_to_all | solution.py:48
  67.9 0.1 copy.42
  67.9 0.1 reshape.89
  68.1 0.0 copy-done.1
  68.1 0.2 convolution_convert_fusion.1
  68.2 0.0 copy-done.2
  68.2 0.3 convolution_convert_fusion.2
  68.6 0.8 broadcast_in_dim.31
  69.3 4.8 %all-to-all-start.2 = ((bf16[8,4,32,128]{3,2,1,0:T(8,128)(2,1)}), bf16[8,4,32,128]{3,2,1,0:T(8,128)(2,1)S(1)}, u32[]{:S(2)}, u32[]{:S(2)}) async-start(bf16[8,4,32,128]{3,2,1,0:T(8,128)(2,1)} %broadcast_in_dim.31), calls=%async_computation.2 | async-start | bytes 524288 | tf_op jit(solution)/shard_map/all_to_all | solution.py:58
  74.2 0.0 copy-done.3
  74.2 7.5 %all-to-all-done.2 = bf16[8,4,32,128]{3,2,1,0:T(8,128)(2,1)S(1)} async-done(((bf16[8,4,32,128]{3,2,1,0:T(8,128)(2,1)}), bf16[8,4,32,128]{3,2,1,0:T(8,128)(2,1)S(1)}, u32[]{:S(2)}, u32[]{:S(2)}) %all-to-all-start.2) | async-done | bytes 262176 | tf_op jit(solution)/shard_map/all_to_all | solution.py:58
  81.7 0.1 fusion.2
  81.9 0.7 broadcast_in_dim.32
  82.6 3.4 %all-to-all-start.3 = ((bf16[8,4,16,128]{3,1,2,0:T(4,128)(2,1)}), bf16[8,4,16,128]{3,1,2,0:T(4,128)(2,1)S(1)}, u32[]{:S(2)}, u32[]{:S(2)}) async-start(bf16[8,4,16,128]{3,1,2,0:T(4,128)(2,1)} %broadcast_in_dim.32), calls=%async_computation.3 | async-start | bytes 262144 | tf_op jit(solution)/shard_map/all_to_all | solution.py:67
  86.0 0.1 slice_convert_fusion
  86.1 0.1 eq.55
  86.2 9.2 %all-to-all-done.3 = bf16[8,4,16,128]{3,1,2,0:T(4,128)(2,1)S(1)} async-done(((bf16[8,4,16,128]{3,1,2,0:T(4,128)(2,1)}), bf16[8,4,16,128]{3,1,2,0:T(4,128)(2,1)S(1)}, u32[]{:S(2)}, u32[]{:S(2)}) %all-to-all-start.3) | async-done | bytes 131104 | tf_op jit(solution)/shard_map/all_to_all | solution.py:67
  95.4 0.2 fusion.6
  95.6 0.7 copy.36
  96.4 3.5 %all-to-all-start.4 = ((f32[12,2,16,128]{3,2,1,0:T(8,128)}), f32[12,2,16,128]{3,2,1,0:T(8,128)S(1)}, u32[]{:S(2)}, u32[]{:S(2)}) async-start(f32[12,2,16,128]{3,2,1,0:T(8,128)} %copy.36), calls=%async_computation.4 | async-start | bytes 393216 | tf_op jit(solution)/shard_map/all_to_all | solution.py:79
  99.9 0.4 convolution_multiply_fusion.1
  100.3 13.5 %all-to-all-done.4 = f32[12,2,16,128]{3,2,1,0:T(8,128)S(1)} async-done(((f32[12,2,16,128]{3,2,1,0:T(8,128)}), f32[12,2,16,128]{3,2,1,0:T(8,128)S(1)}, u32[]{:S(2)}, u32[]{:S(2)}) %all-to-all-start.4) | async-done | bytes 196640 | tf_op jit(solution)/shard_map/all_to_all | solution.py:79
  113.8 0.6 reduce_sum.29
  114.4 0.0 all-gather.2.cloned.1.call-done
  114.4 0.0 copy-done
  114.4 3.1 %fusion.1 = bf16[512,640]{1,0:T(8,128)(2,1)} fusion(f32[512,640]{1,0:T(8,128)S(1)} %bitcast.34, bf16[512,1024]{1,0:T(8,128)(2,1)} %all-gather.2.cloned.1.call-done, bf16[640,1024]{1,0:T(8,128)(2,1)S(1)} %copy-done, f32[512]{0:T(512)S(1)} %get-tuple-element.2), kind=kOutput, calls=%fused_computation.3 | convolution fusion | flops 672071680 | bytes 4327424 | tf_op jit(solution)/shard_map/dot_general | solution.py:84
  (17 shorter events, 0.3 us)
Async XLA Ops:
  7.2 107.2 %copy-start = (bf16[640,1024]{1,0:T(8,128)(2,1)S(1)}, bf16[640,1024]{1,0:T(8,128)(2,1)}, u32[]{:S(2)}) copy-start(bf16[640,1024]{1,0:T(8,128)(2,1)} %param.10) | copy-start | bytes 3932164
  7.2 60.9 %copy-start.1 = (bf16[512,128]{1,0:T(8,128)(2,1)S(1)}, bf16[512,128]{1,0:T(8,128)(2,1)}, u32[]{:S(2)}) copy-start(bf16[512,128]{1,0:T(8,128)(2,1)} %param.9) | copy-start | bytes 393220
  7.2 61.0 %copy-start.2 = (bf16[512,640]{1,0:T(8,128)(2,1)S(1)}, bf16[512,640]{1,0:T(8,128)(2,1)}, u32[]{:S(2)}) copy-start(bf16[512,640]{1,0:T(8,128)(2,1)} %param.8) | copy-start | bytes 1966084
  47.2 20.6 %all-to-all-start.1 = ((bf16[96,4,128]{2,1,0:T(4,128)(2,1)}), bf16[96,4,128]{2,1,0:T(4,128)(2,1)S(1)}, u32[]{:S(2)}, u32[]{:S(2)}) async-start(bf16[96,4,128]{2,1,0:T(4,128)(2,1)} %bitcast.4), calls=%async_computation.1 | async-start | bytes 196608 | tf_op jit(solution)/shard_map/all_to_all | solution.py:48
  53.2 21.0 %copy-start.3 = (s32[512]{0:T(512)S(1)}, s32[512]{0:T(512)}, u32[]{:S(2)}) copy-start(s32[512]{0:T(512)} %param.14) | copy-start | bytes 6148
  53.2 61.2 %all-gather.2.cloned.1.call-start = ((), (), s32[]{:S(2)}) async-start(), calls=%async_computation.5 | async-start | bytes 1179648 | tf_op jit(solution)/shard_map/all_gather | solution.py:29
  69.3 12.3 %all-to-all-start.2 = ((bf16[8,4,32,128]{3,2,1,0:T(8,128)(2,1)}), bf16[8,4,32,128]{3,2,1,0:T(8,128)(2,1)S(1)}, u32[]{:S(2)}, u32[]{:S(2)}) async-start(bf16[8,4,32,128]{3,2,1,0:T(8,128)(2,1)} %broadcast_in_dim.31), calls=%async_computation.2 | async-start | bytes 524288 | tf_op jit(solution)/shard_map/all_to_all | solution.py:58
  82.6 12.8 %all-to-all-start.3 = ((bf16[8,4,16,128]{3,1,2,0:T(4,128)(2,1)}), bf16[8,4,16,128]{3,1,2,0:T(4,128)(2,1)S(1)}, u32[]{:S(2)}, u32[]{:S(2)}) async-start(bf16[8,4,16,128]{3,1,2,0:T(4,128)(2,1)} %broadcast_in_dim.32), calls=%async_computation.3 | async-start | bytes 262144 | tf_op jit(solution)/shard_map/all_to_all | solution.py:67
  96.4 17.4 %all-to-all-start.4 = ((f32[12,2,16,128]{3,2,1,0:T(8,128)}), f32[12,2,16,128]{3,2,1,0:T(8,128)S(1)}, u32[]{:S(2)}, u32[]{:S(2)}) async-start(f32[12,2,16,128]{3,2,1,0:T(8,128)} %copy.36), calls=%async_computation.4 | async-start | bytes 393216 | tf_op jit(solution)/shard_map/all_to_all | solution.py:79
Sparse Core Ops, SparseCore 0:
  56.4 32.6 all-gather.1

commit v2 on v1

--- a/solution.py
+++ b/solution.py
@@ -6,6 +6,7 @@
 adapter_scale_factor = 2.0
 LINE = 8
 LANES = 128
+CORES = 2
 
 
 def on_device(
@@ -26,7 +27,19 @@
     my_y = lax.axis_index("dp") % LINE
     my_row = lax.axis_index("dp") // LINE
 
-    full_cotangent = lax.all_gather(cotangent, "tensor", axis=1, tiled=True)
+    my_tensor = lax.axis_index("tensor")
+    my_x, my_core = my_tensor // CORES, my_tensor % CORES
+    last = tensor - 1
+
+    def both(mine, other, mine_first):
+        return jnp.where(mine_first, jnp.concatenate([mine, other], axis=1), jnp.concatenate([other, mine], axis=1))
+
+    near = [(i, i ^ 1) for i in range(tensor)]
+    pair = [(i, i ^ CORES) for i in range(tensor)]
+    far = [(i, (last - i) ^ 1) for i in range(tensor)]
+    held = both(cotangent, lax.ppermute(cotangent, "tensor", near), my_core == 0)
+    held = both(held, lax.ppermute(held, "tensor", pair), my_x % 2 == 0)
+    full_cotangent = both(held, lax.ppermute(held, "tensor", far), my_x < 2)
 
     matches = block_adapter[:, None] == jnp.arange(nadapt, dtype=jnp.int32)[None, :]
     slot_ids = jnp.sum(jnp.where(matches, owner_map[None, :], 0), axis=1)

time: 125 us -> 107 us (0.86)
  blocking collectives: 36.8 us -> 0 us
  starting transfers between devices: 17.7 us -> 47 us
  between operations: 14.3 us -> 0.93 us
  waiting for transfers between devices: 44.7 us -> 47.1 us
    all_to_all x1 -> x0, blocking collectives: 36.8 us -> none  [on_device(): lax.all_to_all(jnp.concatenate([pieces, id_rows], axis=1), 'dp', 0, 0)]
    all_to_all x0 -> x1, starting transfers between devices: none -> 22 us  [on_device(): lax.all_to_all(jnp.concatenate([pieces, id_rows], axis=1), 'dp', 0, 0)]
    all_to_all x0 -> x1, waiting for transfers between devices: none -> 13 us  [on_device(): lax.all_to_all(jnp.concatenate([pieces, id_rows], axis=1), 'dp', 0, 0)]
    ppermute x0 -> x3, starting transfers between devices: none -> 7.31 us  [the longest x1 3.41 us: on_device(): full_cotangent = both(held, lax.ppermute(held, 'tensor', far), my_x < 2)]
    all_to_all x1, waiting for transfers between devices: 13.5 us -> 8.33 us  [on_device(): lax.all_to_all(sums.reshape(columns, own_slots, rank, kpiece), 'dp', 0, 0...]
    all_to_all x1, waiting for transfers between devices: 9.16 us -> 5.24 us  [on_device(): lax.all_to_all(jnp.broadcast_to(terms, (LINE,) + terms.shape), 'dp', 0, 0...]
    all_to_all x1, waiting for transfers between devices: 7.46 us -> 4.37 us  [on_device(): lax.all_to_all(jnp.broadcast_to(part, (tensor,) + part.shape), 'tensor',...]
    ppermute x0 -> x3, waiting for transfers between devices: none -> 1.58 us  [the longest x1 1.57 us: on_device(): full_cotangent = both(held, lax.ppermute(held, 'tensor', far), my_x < 2)]
  transfers between devices with their start and end apart: 5 -> 8, of which waited for: 4 -> 6; matrix products, arithmetic and copies ran while one was open for 4% -> 8% of each run, Pallas kernels for 0% -> 0%
where the time goes in v2:
time: 107 us
  waiting for transfers between devices  47.1 us (44%)
  starting transfers between devices  47 us (44%)
  matrix products  5.21 us (5%)
  local copies, waits for them, and re-layouts  3.53 us (3%)
  other arithmetic  3 us (3%)
    all_to_all x1, starting transfers between devices, on_device(): lax.all_to_all(jnp.concatenate([pieces, id_rows], axis=1), 'dp', 0, 0)  22 us
    all_to_all x1, waiting for transfers between devices, on_device(): picked = lax.all_to_all(picked.reshape(dp, block_count, LANES), 'dp', 0, 0)  14.6 us
    all_to_all x1, waiting for transfers between devices, on_device(): lax.all_to_all(jnp.concatenate([pieces, id_rows], axis=1), 'dp', 0, 0)  13 us
    all_to_all x1, waiting for transfers between devices, on_device(): lax.all_to_all(sums.reshape(columns, own_slots, rank, kpiece), 'dp', 0, 0...  8.33 us
    all_to_all x1, starting transfers between devices, on_device(): picked = lax.all_to_all(picked.reshape(dp, block_count, LANES), 'dp', 0, 0)  5.94 us
    all_to_all x1, waiting for transfers between devices, on_device(): lax.all_to_all(jnp.broadcast_to(terms, (LINE,) + terms.shape), 'dp', 0, 0...  5.24 us
    all_to_all x1, starting transfers between devices, on_device(): lax.all_to_all(jnp.broadcast_to(part, (tensor,) + part.shape), 'tensor',...  4.83 us
    all_to_all x1, waiting for transfers between devices, on_device(): lax.all_to_all(jnp.broadcast_to(part, (tensor,) + part.shape), 'tensor',...  4.37 us
  transfers between devices with their start and end apart: 8, of which 6 were waited for; matrix products, arithmetic and copies ran while one was open for 8% of the time, Pallas kernels for 0%

profile of v2, /device:TPU:2, one launch (start us, length us, event | category | flops | bytes accessed | tf_op | source)
XLA Modules:
  0.0 106.8 jit_solution(9015206558603582407)
XLA Ops:
  0.6 0.0 copy-start
  0.6 0.0 copy-start.1
  0.7 0.0 copy-start.3
  0.7 0.0 copy-start.2
  0.7 1.0 select_reduce_fusion
  1.7 0.8 pad_maximum_fusion.1
  2.5 0.1 reshape.85
  2.6 0.7 copy.31
  3.3 22.0 %all-to-all-start = ((bf16[96,4,128]{2,1,0:T(4,128)(2,1)}), bf16[96,4,128]{2,1,0:T(4,128)(2,1)S(1)}, u32[]{:S(2)}, u32[]{:S(2)}) async-start(bf16[96,4,128]{2,1,0:T(4,128)(2,1)} %copy.31), calls=%async_computation | async-start | bytes 196608 | tf_op jit(solution)/shard_map/all_to_all | solution.py:53
  25.3 1.9 %collective-permute-start = (bf16[512,128]{1,0:T(8,128)(2,1)}, bf16[512,128]{1,0:T(8,128)(2,1)S(1)}, u32[]{:S(2)}, u32[]{:S(2)}) collective-permute-start(bf16[512,128]{1,0:T(8,128)(2,1)} %param.9), channel_id=1, source_target_pairs={{0,1},{1,0},{2,3},{3,2},{4,5},{5,4},{6,7},{7,6},{8,9},{9,8},{10,11... | collective-permute-start | bytes 393224 | tf_op jit(solution)/shard_map/ppermute | solution.py:40
  27.3 13.0 %all-to-all-done = bf16[96,4,128]{2,1,0:T(4,128)(2,1)S(1)} async-done(((bf16[96,4,128]{2,1,0:T(4,128)(2,1)}), bf16[96,4,128]{2,1,0:T(4,128)(2,1)S(1)}, u32[]{:S(2)}, u32[]{:S(2)}) %all-to-all-start) | async-done | bytes 98336 | tf_op jit(solution)/shard_map/all_to_all | solution.py:53
  40.3 0.2 fusion.19
  40.5 0.1 reshape.93
  40.7 0.9 convolution_convert_fusion
  41.6 5.9 %all-to-all-start.1 = ((bf16[96,4,128]{2,1,0:T(4,128)(2,1)}), bf16[96,4,128]{2,1,0:T(4,128)(2,1)S(1)}, u32[]{:S(2)}, u32[]{:S(2)}) async-start(bf16[96,4,128]{2,1,0:T(4,128)(2,1)} %bitcast.4), calls=%async_computation.1 | async-start | bytes 196608 | tf_op jit(solution)/shard_map/all_to_all | solution.py:61
  47.5 0.0 copy-done.3
  47.5 14.6 %all-to-all-done.1 = bf16[96,4,128]{2,1,0:T(4,128)(2,1)S(1)} async-done(((bf16[96,4,128]{2,1,0:T(4,128)(2,1)}), bf16[96,4,128]{2,1,0:T(4,128)(2,1)S(1)}, u32[]{:S(2)}, u32[]{:S(2)}) %all-to-all-start.1) | async-done | bytes 98336 | tf_op jit(solution)/shard_map/all_to_all | solution.py:61
  62.2 0.1 copy.42
  62.2 0.1 reshape.89
  62.4 0.0 copy-done.1
  62.4 0.2 convolution_convert_fusion.1
  62.5 0.0 copy-done.2
  62.5 0.3 convolution_convert_fusion.2
  62.9 0.8 broadcast_in_dim.31
  63.6 4.8 %all-to-all-start.2 = ((bf16[8,4,32,128]{3,2,1,0:T(8,128)(2,1)}), bf16[8,4,32,128]{3,2,1,0:T(8,128)(2,1)S(1)}, u32[]{:S(2)}, u32[]{:S(2)}) async-start(bf16[8,4,32,128]{3,2,1,0:T(8,128)(2,1)} %broadcast_in_dim.31), calls=%async_computation.2 | async-start | bytes 524288 | tf_op jit(solution)/shard_map/all_to_all | solution.py:71
  68.5 0.0 collective-permute-done
  68.5 0.1 maximum_select_fusion.3
  68.6 2.0 %collective-permute-start.1 = (bf16[512,256]{1,0:T(8,128)(2,1)S(1)}, bf16[512,256]{1,0:T(8,128)(2,1)S(1)}, u32[]{:S(2)}, u32[]{:S(2)}) collective-permute-start(bf16[512,256]{1,0:T(8,128)(2,1)S(1)} %maximum_select_fusion.3), channel_id=1, source_target_pairs={{0,2},{1,3},{2,0},{3,1},{4,6},{5,7},{6,4},{7,5},{8,10},{9,11},{10,... | collective-permute-start | bytes 786440 | tf_op jit(solution)/shard_map/ppermute | solution.py:41
  70.6 4.4 %all-to-all-done.2 = bf16[8,4,32,128]{3,2,1,0:T(8,128)(2,1)S(1)} async-done(((bf16[8,4,32,128]{3,2,1,0:T(8,128)(2,1)}), bf16[8,4,32,128]{3,2,1,0:T(8,128)(2,1)S(1)}, u32[]{:S(2)}, u32[]{:S(2)}) %all-to-all-start.2) | async-done | bytes 262176 | tf_op jit(solution)/shard_map/all_to_all | solution.py:71
  75.0 0.1 fusion.2
  75.2 0.7 broadcast_in_dim.32
  75.9 3.4 %all-to-all-start.3 = ((bf16[8,4,16,128]{3,1,2,0:T(4,128)(2,1)}), bf16[8,4,16,128]{3,1,2,0:T(4,128)(2,1)S(1)}, u32[]{:S(2)}, u32[]{:S(2)}) async-start(bf16[8,4,16,128]{3,1,2,0:T(4,128)(2,1)} %broadcast_in_dim.32), calls=%async_computation.3 | async-start | bytes 262144 | tf_op jit(solution)/shard_map/all_to_all | solution.py:80
  79.2 0.0 collective-permute-done.1
  79.2 0.1 maximum_select_fusion.2
  79.4 3.4 %collective-permute-start.2 = (bf16[512,512]{1,0:T(8,128)(2,1)S(1)}, bf16[512,512]{1,0:T(8,128)(2,1)}, u32[]{:S(2)}, u32[]{:S(2)}) collective-permute-start(bf16[512,512]{1,0:T(8,128)(2,1)S(1)} %maximum_select_fusion.2), channel_id=1, source_target_pairs={{0,6},{1,7},{2,4},{3,5},{4,2},{5,3},{6,0},{7,1},{8,14},{9,15},{10,... | collective-permute-start | bytes 1572872 | tf_op jit(solution)/shard_map/ppermute | solution.py:42
  82.8 0.1 slice_convert_fusion
  82.9 0.1 eq.65
  83.0 5.2 %all-to-all-done.3 = bf16[8,4,16,128]{3,1,2,0:T(4,128)(2,1)S(1)} async-done(((bf16[8,4,16,128]{3,1,2,0:T(4,128)(2,1)}), bf16[8,4,16,128]{3,1,2,0:T(4,128)(2,1)S(1)}, u32[]{:S(2)}, u32[]{:S(2)}) %all-to-all-start.3) | async-done | bytes 131104 | tf_op jit(solution)/shard_map/all_to_all | solution.py:80
  88.3 0.2 fusion.12
  88.5 0.7 copy.36
  89.2 3.5 %all-to-all-start.4 = ((f32[12,2,16,128]{3,2,1,0:T(8,128)}), f32[12,2,16,128]{3,2,1,0:T(8,128)S(1)}, u32[]{:S(2)}, u32[]{:S(2)}) async-start(f32[12,2,16,128]{3,2,1,0:T(8,128)} %copy.36), calls=%async_computation.4 | async-start | bytes 393216 | tf_op jit(solution)/shard_map/all_to_all | solution.py:92
  92.8 0.4 convolution_multiply_fusion.1
  93.2 1.6 %collective-permute-done.2 = bf16[512,512]{1,0:T(8,128)(2,1)} collective-permute-done((bf16[512,512]{1,0:T(8,128)(2,1)S(1)}, bf16[512,512]{1,0:T(8,128)(2,1)}, u32[]{:S(2)}, u32[]{:S(2)}) %collective-permute-start.2) | collective-permute-done | bytes 524320 | tf_op jit(solution)/shard_map/ppermute | solution.py:42
  94.7 0.0 copy-done
  94.7 3.1 %fusion.1 = bf16[512,640]{1,0:T(8,128)(2,1)} fusion(f32[512,640]{1,0:T(8,128)S(1)} %bitcast.33, bf16[640,1024]{1,0:T(8,128)(2,1)S(1)} %copy-done, bf16[512,512]{1,0:T(8,128)(2,1)} %collective-permute-done.2, bf16[512,512]{1,0:T(8,128)(2,1)S(1)} %maximum_select_fusion.2, pred[]{:T(512)S(6)} %lt.20, f32[512]{0:T(512)S(1)} %get-tuple-element.2), kind=kOutput, calls=%fused_computation.3 | convolution fusion | flops 676790272 | bytes 4327425 | tf_op jit(solution)/shard_map/dot_general | solution.py:97
  97.8 8.3 %all-to-all-done.4 = f32[12,2,16,128]{3,2,1,0:T(8,128)S(1)} async-done(((f32[12,2,16,128]{3,2,1,0:T(8,128)}), f32[12,2,16,128]{3,2,1,0:T(8,128)S(1)}, u32[]{:S(2)}, u32[]{:S(2)}) %all-to-all-start.4) | async-done | bytes 196640 | tf_op jit(solution)/shard_map/all_to_all | solution.py:92
  106.1 0.6 reduce_sum.29
  (17 shorter events, 0.3 us)
Async XLA Ops:
  0.6 94.1 %copy-start = (bf16[640,1024]{1,0:T(8,128)(2,1)S(1)}, bf16[640,1024]{1,0:T(8,128)(2,1)}, u32[]{:S(2)}) copy-start(bf16[640,1024]{1,0:T(8,128)(2,1)} %param.10) | copy-start | bytes 3932164
  0.6 61.7 %copy-start.1 = (bf16[512,128]{1,0:T(8,128)(2,1)S(1)}, bf16[512,128]{1,0:T(8,128)(2,1)}, u32[]{:S(2)}) copy-start(bf16[512,128]{1,0:T(8,128)(2,1)} %param.9) | copy-start | bytes 393220
  0.7 46.9 %copy-start.3 = (s32[512]{0:T(512)S(1)}, s32[512]{0:T(512)}, u32[]{:S(2)}) copy-start(s32[512]{0:T(512)} %param.14) | copy-start | bytes 6148
  0.7 61.9 %copy-start.2 = (bf16[512,640]{1,0:T(8,128)(2,1)S(1)}, bf16[512,640]{1,0:T(8,128)(2,1)}, u32[]{:S(2)}) copy-start(bf16[512,640]{1,0:T(8,128)(2,1)} %param.8) | copy-start | bytes 1966084
  3.3 37.0 %all-to-all-start = ((bf16[96,4,128]{2,1,0:T(4,128)(2,1)}), bf16[96,4,128]{2,1,0:T(4,128)(2,1)S(1)}, u32[]{:S(2)}, u32[]{:S(2)}) async-start(bf16[96,4,128]{2,1,0:T(4,128)(2,1)} %copy.31), calls=%async_computation | async-start | bytes 196608 | tf_op jit(solution)/shard_map/all_to_all | solution.py:53
  25.3 43.1 %collective-permute-start = (bf16[512,128]{1,0:T(8,128)(2,1)}, bf16[512,128]{1,0:T(8,128)(2,1)S(1)}, u32[]{:S(2)}, u32[]{:S(2)}) collective-permute-start(bf16[512,128]{1,0:T(8,128)(2,1)} %param.9), channel_id=1, source_target_pairs={{0,1},{1,0},{2,3},{3,2},{4,5},{5,4},{6,7},{7,6},{8,9},{9,8},{10,11... | collective-permute-start | bytes 393224 | tf_op jit(solution)/shard_map/ppermute | solution.py:40
  41.6 20.6 %all-to-all-start.1 = ((bf16[96,4,128]{2,1,0:T(4,128)(2,1)}), bf16[96,4,128]{2,1,0:T(4,128)(2,1)S(1)}, u32[]{:S(2)}, u32[]{:S(2)}) async-start(bf16[96,4,128]{2,1,0:T(4,128)(2,1)} %bitcast.4), calls=%async_computation.1 | async-start | bytes 196608 | tf_op jit(solution)/shard_map/all_to_all | solution.py:61
  63.6 11.3 %all-to-all-start.2 = ((bf16[8,4,32,128]{3,2,1,0:T(8,128)(2,1)}), bf16[8,4,32,128]{3,2,1,0:T(8,128)(2,1)S(1)}, u32[]{:S(2)}, u32[]{:S(2)}) async-start(bf16[8,4,32,128]{3,2,1,0:T(8,128)(2,1)} %broadcast_in_dim.31), calls=%async_computation.2 | async-start | bytes 524288 | tf_op jit(solution)/shard_map/all_to_all | solution.py:71
  68.6 10.7 %collective-permute-start.1 = (bf16[512,256]{1,0:T(8,128)(2,1)S(1)}, bf16[512,256]{1,0:T(8,128)(2,1)S(1)}, u32[]{:S(2)}, u32[]{:S(2)}) collective-permute-start(bf16[512,256]{1,0:T(8,128)(2,1)S(1)} %maximum_select_fusion.3), channel_id=1, source_target_pairs={{0,2},{1,3},{2,0},{3,1},{4,6},{5,7},{6,4},{7,5},{8,10},{9,11},{10,... | collective-permute-start | bytes 786440 | tf_op jit(solution)/shard_map/ppermute | solution.py:41
  75.9 12.4 %all-to-all-start.3 = ((bf16[8,4,16,128]{3,1,2,0:T(4,128)(2,1)}), bf16[8,4,16,128]{3,1,2,0:T(4,128)(2,1)S(1)}, u32[]{:S(2)}, u32[]{:S(2)}) async-start(bf16[8,4,16,128]{3,1,2,0:T(4,128)(2,1)} %broadcast_in_dim.32), calls=%async_computation.3 | async-start | bytes 262144 | tf_op jit(solution)/shard_map/all_to_all | solution.py:80
  79.4 15.4 %collective-permute-start.2 = (bf16[512,512]{1,0:T(8,128)(2,1)S(1)}, bf16[512,512]{1,0:T(8,128)(2,1)}, u32[]{:S(2)}, u32[]{:S(2)}) collective-permute-start(bf16[512,512]{1,0:T(8,128)(2,1)S(1)} %maximum_select_fusion.2), channel_id=1, source_target_pairs={{0,6},{1,7},{2,4},{3,5},{4,2},{5,3},{6,0},{7,1},{8,14},{9,15},{10,... | collective-permute-start | bytes 1572872 | tf_op jit(solution)/shard_map/ppermute | solution.py:42
  89.2 16.9 %all-to-all-start.4 = ((f32[12,2,16,128]{3,2,1,0:T(8,128)}), f32[12,2,16,128]{3,2,1,0:T(8,128)S(1)}, u32[]{:S(2)}, u32[]{:S(2)}) async-start(f32[12,2,16,128]{3,2,1,0:T(8,128)} %copy.36), calls=%async_computation.4 | async-start | bytes 393216 | tf_op jit(solution)/shard_map/all_to_all | solution.py:92

commit v3 on v2

--- a/solution.py
+++ b/solution.py
@@ -1,12 +1,50 @@
 import jax
 import jax.numpy as jnp
 from jax import lax
+from jax.experimental import pallas as pl
+from jax.experimental.pallas import tpu as pltpu
 from jax.sharding import PartitionSpec as P
 
 adapter_scale_factor = 2.0
 LINE = 8
 LANES = 128
 CORES = 2
+
+
+SPARE = 4
+
+
+def pack_kernel(adapter_ref, owner_ref, down_ref, up_ref, out_ref):
+    slots, rank, dpiece = down_ref.shape
+    blocks = adapter_ref.shape[0]
+    rows = rank * SPARE
+    at = lax.broadcasted_iota(jnp.int32, (rows, slots * rank), 0)
+    source = lax.broadcasted_iota(jnp.int32, (rows, slots * rank), 1)
+    spread = (source == (at % SPARE) * rank + at // SPARE).astype(jnp.bfloat16)
+    kind = lax.broadcasted_iota(jnp.int32, (rows, LANES), 0) % SPARE
+    lane = lax.broadcasted_iota(jnp.int32, (rows, LANES), 1)
+    numbers = jnp.zeros((rows, LANES), jnp.float32)
+    for b in range(blocks):
+        slot = owner_ref[adapter_ref[b]].astype(jnp.float32)
+        numbers = jnp.where((kind == slots) & (lane == b), slot, numbers)
+    down = jnp.concatenate([down_ref[j] for j in range(slots)], axis=0)
+    up = jnp.concatenate([up_ref[j] for j in range(slots)], axis=0)
+    for c in range(dpiece // LANES + 1):
+        chunk = up if c == dpiece // LANES else down[:, c * LANES : (c + 1) * LANES]
+        mixed = jnp.dot(spread, chunk, preferred_element_type=jnp.float32)
+        out_ref[c * rows : (c + 1) * rows, :] = (mixed + numbers).astype(jnp.bfloat16)
+
+
+def pack(block_adapter, owner_map, down_rows, up_b):
+    _, rank, dpiece = down_rows.shape
+    smem = pl.BlockSpec(memory_space=pltpu.SMEM)
+    vmem = pl.BlockSpec(memory_space=pltpu.VMEM)
+    return pl.pallas_call(
+        pack_kernel,
+        out_shape=jax.ShapeDtypeStruct((SPARE * rank * (dpiece // LANES + 1), LANES), jnp.bfloat16),
+        in_specs=[smem, smem, vmem, vmem],
+        out_specs=vmem,
+    )(block_adapter, owner_map, down_rows, up_b)
 
 
 def on_device(
@@ -16,7 +54,6 @@
     kpiece = cotangent.shape[1]
     block_count = block_adapter.shape[0]
     blk_rows = row_count // block_count
-    nadapt = owner_map.shape[0]
     own_slots, _, rank = down_a.shape
     dp = lax.axis_size("dp")
     tensor = lax.axis_size("tensor")
@@ -41,16 +78,10 @@
     held = both(held, lax.ppermute(held, "tensor", pair), my_x % 2 == 0)
     full_cotangent = both(held, lax.ppermute(held, "tensor", far), my_x < 2)
 
-    matches = block_adapter[:, None] == jnp.arange(nadapt, dtype=jnp.int32)[None, :]
-    slot_ids = jnp.sum(jnp.where(matches, owner_map[None, :], 0), axis=1)
     live = (token_adapter >= 0).astype(jnp.float32)
 
-    weights = jnp.concatenate([down_a.transpose(0, 2, 1), up_b], axis=2)
-    pieces = weights.reshape(own_slots, rank, chunks + 1, LANES).transpose(2, 1, 0, 3)
-    pieces = pieces.reshape(dp, own_slots, LANES)
-    id_row = jnp.pad(slot_ids, (0, LANES - block_count)).astype(jnp.bfloat16)
-    id_rows = jnp.broadcast_to(id_row, (dp, own_slots, LANES))
-    table = lax.all_to_all(jnp.concatenate([pieces, id_rows], axis=1), "dp", 0, 0)
+    pieces = pack(block_adapter, owner_map, down_a.transpose(0, 2, 1), up_b)
+    table = lax.all_to_all(pieces.reshape(dp, SPARE, LANES), "dp", 0, 0)
     all_slots = table[:, own_slots, :block_count].astype(jnp.int32)
     table = table[:, :own_slots].reshape(dp * own_slots, LANES)
 
@@ -90,9 +121,9 @@
     owner_match = (column_slots[:, None] == row_slots[None, :]).astype(jnp.bfloat16)
     sums = jnp.einsum("sb,bro->sro", owner_match, terms, preferred_element_type=jnp.float32)
     sums = lax.all_to_all(
-        sums.reshape(columns, own_slots, rank, kpiece), "dp", 0, 0, axis_index_groups=z_groups
+        sums.astype(jnp.bfloat16).reshape(columns, own_slots, rank, kpiece), "dp", 0, 0, axis_index_groups=z_groups
     )
-    grad_b = jnp.sum(sums, axis=0)
+    grad_b = jnp.sum(sums.astype(jnp.float32), axis=0)
 
     frozen = lax.dot_general(
         full_cotangent, base_weight, (((1,), (1,)), ((), ())), preferred_element_type=jnp.float32

time: 107 us -> 104 us (0.972)
  waiting for transfers between devices: 47.1 us -> 41.6 us
  Pallas kernels: 0 us -> 1.73 us
    all_to_all x1, waiting for transfers between devices: 14.6 us -> 10.4 us  [on_device(): picked = lax.all_to_all(picked.reshape(dp, block_count, LANES), 'dp', 0, 0)]
    all_to_all x1, waiting for transfers between devices: 5.24 us -> 8.61 us  [on_device(): lax.all_to_all(jnp.broadcast_to(terms, (LINE,) + terms.shape), 'dp', 0, 0...]
    all_to_all x1, waiting for transfers between devices: 4.37 us -> 1.35 us  [on_device(): lax.all_to_all(jnp.broadcast_to(part, (tensor,) + part.shape), 'tensor',...]
    select_n x2, other arithmetic: 0.21 us -> 2.21 us  [both(): jnp.where(mine_first, jnp.concatenate([mine, other], axis=1), jnp.concate...]
    pallas_call x0 -> x1, Pallas kernels: none -> 1.73 us  [pack(): pl.pallas_call(pack_kernel, out_shape=jax.ShapeDtypeStruct((SPARE * rank...]
    ppermute x1, waiting for transfers between devices: 1.57 us -> 0.01 us  [on_device(): full_cotangent = both(held, lax.ppermute(held, 'tensor', far), my_x < 2)]
  transfers between devices with their start and end apart: 8 -> 8, of which waited for: 6 -> 5; matrix products, arithmetic and copies ran while one was open for 8% -> 11% of each run, Pallas kernels for 0% -> 0%
where the time goes in v3:
time: 104 us
  starting transfers between devices  47.4 us (46%)
  waiting for transfers between devices  41.6 us (40%)
  matrix products  5.2 us (5%)
  other arithmetic  3.92 us (4%)
  local copies, waits for them, and re-layouts  2.78 us (3%)
  Pallas kernels  1.73 us (2%)
    all_to_all x1, starting transfers between devices, on_device(): table = lax.all_to_all(pieces.reshape(dp, SPARE, LANES), 'dp', 0, 0)  22 us
    all_to_all x1, waiting for transfers between devices, on_device(): table = lax.all_to_all(pieces.reshape(dp, SPARE, LANES), 'dp', 0, 0)  12.8 us
    all_to_all x1, waiting for transfers between devices, on_device(): picked = lax.all_to_all(picked.reshape(dp, block_count, LANES), 'dp', 0, 0)  10.4 us
    all_to_all x1, waiting for transfers between devices, on_device(): lax.all_to_all(jnp.broadcast_to(terms, (LINE,) + terms.shape), 'dp', 0, 0...  8.61 us
    all_to_all x1, waiting for transfers between devices, on_device(): lax.all_to_all(sums.astype(jnp.bfloat16).reshape(columns, own_slots, rank...  8.44 us
    all_to_all x1, starting transfers between devices, on_device(): picked = lax.all_to_all(picked.reshape(dp, block_count, LANES), 'dp', 0, 0)  5.94 us
    all_to_all x1, starting transfers between devices, on_device(): lax.all_to_all(jnp.broadcast_to(part, (tensor,) + part.shape), 'tensor',...  4.83 us
    all_to_all x1, starting transfers between devices, on_device(): lax.all_to_all(sums.astype(jnp.bfloat16).reshape(columns, own_slots, rank...  3.51 us
  transfers between devices with their start and end apart: 8, of which 5 were waited for; matrix products, arithmetic and copies ran while one was open for 11% of the time, Pallas kernels for 0%

profile of v3, /device:TPU:2, one launch (start us, length us, event | category | flops | bytes accessed | tf_op | source)
XLA Modules:
  0.0 103.6 jit_solution(1744005809557038518)
XLA Ops:
  0.6 0.0 copy-start
  0.6 0.0 copy-start.1
  0.7 0.0 copy-start.2
  0.7 1.7 %shard_map.95 = bf16[384,128]{1,0:T(8,128)(2,1)} custom-call(s32[4]{0:T(128)} %adapter_ref.1, s32[192]{0:T(256)} %owner_ref.1, bf16[2,16,640]{2,1,0:T(8,128)(2,1)} %bitcast.39, bf16[2,16,128]{2,1,0:T(8,128)(2,1)} %up_ref.1), custom_call_target="tpu_custom_call" | custom-call | tf_op jit(solution)/shard_map/pallas_call | solution.py:42
  2.4 22.0 %all-to-all-start = ((bf16[96,4,128]{2,1,0:T(4,128)(2,1)}), bf16[96,4,128]{2,1,0:T(4,128)(2,1)S(1)}, u32[]{:S(2)}, u32[]{:S(2)}) async-start(bf16[96,4,128]{2,1,0:T(4,128)(2,1)} %bitcast.35), calls=%async_computation | async-start | bytes 196608 | tf_op jit(solution)/shard_map/all_to_all | solution.py:84
  24.4 1.9 %collective-permute-start = (bf16[512,128]{1,0:T(8,128)(2,1)}, bf16[512,128]{1,0:T(8,128)(2,1)S(1)}, u32[]{:S(2)}, u32[]{:S(2)}) collective-permute-start(bf16[512,128]{1,0:T(8,128)(2,1)} %param.9), channel_id=1, source_target_pairs={{0,1},{1,0},{2,3},{3,2},{4,5},{5,4},{6,7},{7,6},{8,9},{9,8},{10,11... | collective-permute-start | bytes 393224 | tf_op jit(solution)/shard_map/ppermute | solution.py:77
  26.4 0.1 iota_add_fusion
  26.5 0.1 add.58
  26.6 12.8 %all-to-all-done = bf16[96,4,128]{2,1,0:T(4,128)(2,1)S(1)} async-done(((bf16[96,4,128]{2,1,0:T(4,128)(2,1)}), bf16[96,4,128]{2,1,0:T(4,128)(2,1)S(1)}, u32[]{:S(2)}, u32[]{:S(2)}) %all-to-all-start) | async-done | bytes 98336 | tf_op jit(solution)/shard_map/all_to_all | solution.py:84
  39.4 0.2 fusion.18
  39.6 0.1 reshape.79
  39.7 0.9 convolution_convert_fusion.1
  40.6 5.9 %all-to-all-start.1 = ((bf16[96,4,128]{2,1,0:T(4,128)(2,1)}), bf16[96,4,128]{2,1,0:T(4,128)(2,1)S(1)}, u32[]{:S(2)}, u32[]{:S(2)}) async-start(bf16[96,4,128]{2,1,0:T(4,128)(2,1)} %bitcast.3), calls=%async_computation.1 | async-start | bytes 196608 | tf_op jit(solution)/shard_map/all_to_all | solution.py:92
  46.6 0.7 compare_convert_fusion
  47.3 0.0 collective-permute-done
  47.3 1.1 %maximum_select_fusion.3 = bf16[512,256]{1,0:T(8,128)(2,1)S(1)} fusion(bf16[512,128]{1,0:T(8,128)(2,1)S(1)} %collective-permute-done, bf16[512,128]{1,0:T(8,128)(2,1)} %param.9, pred[]{:T(512)S(6)} %eq.39), kind=kLoop, calls=%fused_computation.20 | loop fusion | flops 1179648 | bytes 524289 | tf_op jit(solution)/shard_map/jit(_where)/select_n | solution.py:72
  48.3 2.4 %collective-permute-start.1 = (bf16[512,256]{1,0:T(8,128)(2,1)S(1)}, bf16[512,256]{1,0:T(8,128)(2,1)}, u32[]{:S(2)}, u32[]{:S(2)}) collective-permute-start(bf16[512,256]{1,0:T(8,128)(2,1)S(1)} %maximum_select_fusion.3), channel_id=1, source_target_pairs={{0,2},{1,3},{2,0},{3,1},{4,6},{5,7},{6,4},{7,5},{8,10},{9,11},{10,... | collective-permute-start | bytes 786440 | tf_op jit(solution)/shard_map/ppermute | solution.py:78
  50.8 10.4 %all-to-all-done.1 = bf16[96,4,128]{2,1,0:T(4,128)(2,1)S(1)} async-done(((bf16[96,4,128]{2,1,0:T(4,128)(2,1)}), bf16[96,4,128]{2,1,0:T(4,128)(2,1)S(1)}, u32[]{:S(2)}, u32[]{:S(2)}) %all-to-all-start.1) | async-done | bytes 98336 | tf_op jit(solution)/shard_map/all_to_all | solution.py:92
  61.2 0.1 copy.47
  61.3 0.1 reshape.74
  61.4 0.0 copy-done.1
  61.4 0.2 convolution_convert_fusion.2
  61.6 0.0 copy-done.2
  61.6 0.3 convolution_convert_fusion.3
  61.9 0.8 broadcast_in_dim.4
  62.7 4.8 %all-to-all-start.2 = ((bf16[8,4,32,128]{3,2,1,0:T(8,128)(2,1)}), bf16[8,4,32,128]{3,2,1,0:T(8,128)(2,1)S(1)}, u32[]{:S(2)}, u32[]{:S(2)}) async-start(bf16[8,4,32,128]{3,2,1,0:T(8,128)(2,1)} %broadcast_in_dim.4), calls=%async_computation.2 | async-start | bytes 524288 | tf_op jit(solution)/shard_map/all_to_all | solution.py:102
  67.5 0.1 slice_convert_fusion
  67.7 0.1 eq.44
  67.7 0.0 collective-permute-done.1
  67.7 1.2 %maximum_select_fusion.2 = bf16[512,512]{1,0:T(8,128)(2,1)S(1)} fusion(bf16[512,256]{1,0:T(8,128)(2,1)} %collective-permute-done.1, bf16[512,256]{1,0:T(8,128)(2,1)S(1)} %maximum_select_fusion.3, pred[]{:T(512)S(6)} %eq.38), kind=kLoop, calls=%fused_computation.17 | loop fusion | flops 2359296 | bytes 1048577 | tf_op jit(solution)/shard_map/jit(_where)/select_n | solution.py:72
  68.9 3.4 %collective-permute-start.2 = (bf16[512,512]{1,0:T(8,128)(2,1)S(1)}, bf16[512,512]{1,0:T(8,128)(2,1)}, u32[]{:S(2)}, u32[]{:S(2)}) collective-permute-start(bf16[512,512]{1,0:T(8,128)(2,1)S(1)} %maximum_select_fusion.2), channel_id=1, source_target_pairs={{0,6},{1,7},{2,4},{3,5},{4,2},{5,3},{6,0},{7,1},{8,14},{9,15},{10,... | collective-permute-start | bytes 1572872 | tf_op jit(solution)/shard_map/ppermute | solution.py:79
  72.3 1.3 %all-to-all-done.2 = bf16[8,4,32,128]{3,2,1,0:T(8,128)(2,1)S(1)} async-done(((bf16[8,4,32,128]{3,2,1,0:T(8,128)(2,1)}), bf16[8,4,32,128]{3,2,1,0:T(8,128)(2,1)S(1)}, u32[]{:S(2)}, u32[]{:S(2)}) %all-to-all-start.2) | async-done | bytes 262176 | tf_op jit(solution)/shard_map/all_to_all | solution.py:102
  73.7 0.1 fusion.2
  73.9 0.7 broadcast_in_dim.5
  74.5 3.4 %all-to-all-start.3 = ((bf16[8,4,16,128]{3,1,2,0:T(4,128)(2,1)}), bf16[8,4,16,128]{3,1,2,0:T(4,128)(2,1)S(1)}, u32[]{:S(2)}, u32[]{:S(2)}) async-start(bf16[8,4,16,128]{3,1,2,0:T(4,128)(2,1)} %broadcast_in_dim.5), calls=%async_computation.3 | async-start | bytes 262144 | tf_op jit(solution)/shard_map/all_to_all | solution.py:111
  77.9 0.4 convolution_multiply_fusion.1
  78.3 8.6 %all-to-all-done.3 = bf16[8,4,16,128]{3,1,2,0:T(4,128)(2,1)S(1)} async-done(((bf16[8,4,16,128]{3,1,2,0:T(4,128)(2,1)}), bf16[8,4,16,128]{3,1,2,0:T(4,128)(2,1)S(1)}, u32[]{:S(2)}, u32[]{:S(2)}) %all-to-all-start.3) | async-done | bytes 131104 | tf_op jit(solution)/shard_map/all_to_all | solution.py:111
  87.0 0.2 convolution_convert_fusion
  87.2 0.7 copy.37
  87.9 3.5 %all-to-all-start.4 = ((bf16[12,2,16,128]{3,1,2,0:T(2,128)(2,1)}), bf16[12,2,16,128]{3,1,2,0:T(2,128)(2,1)S(1)}, u32[]{:S(2)}, u32[]{:S(2)}) async-start(bf16[12,2,16,128]{3,1,2,0:T(2,128)(2,1)} %copy.37), calls=%async_computation.4 | async-start | bytes 196608 | tf_op jit(solution)/shard_map/all_to_all | solution.py:123
  91.4 0.0 collective-permute-done.2
  91.4 0.0 copy-done
  91.4 3.1 %fusion.1 = bf16[512,640]{1,0:T(8,128)(2,1)} fusion(f32[512,640]{1,0:T(8,128)S(1)} %bitcast.29, bf16[640,1024]{1,0:T(8,128)(2,1)S(1)} %copy-done, bf16[512,512]{1,0:T(8,128)(2,1)} %collective-permute-done.2, bf16[512,512]{1,0:T(8,128)(2,1)S(1)} %maximum_select_fusion.2, pred[]{:T(512)S(6)} %lt.20, f32[512]{0:T(512)S(1)} %get-tuple-element.8), kind=kOutput, calls=%fused_computation.3 | convolution fusion | flops 676790272 | bytes 4327425 | tf_op jit(solution)/shard_map/dot_general | solution.py:128
  94.5 8.4 %all-to-all-done.4 = bf16[12,2,16,128]{3,1,2,0:T(2,128)(2,1)S(1)} async-done(((bf16[12,2,16,128]{3,1,2,0:T(2,128)(2,1)}), bf16[12,2,16,128]{3,1,2,0:T(2,128)(2,1)S(1)}, u32[]{:S(2)}, u32[]{:S(2)}) %all-to-all-start.4) | async-done | bytes 98336 | tf_op jit(solution)/shard_map/all_to_all | solution.py:123
  103.0 0.6 convert_reduce_fusion.1
  (10 shorter events, 0.2 us)
Async XLA Ops:
  0.6 90.8 %copy-start = (bf16[640,1024]{1,0:T(8,128)(2,1)S(1)}, bf16[640,1024]{1,0:T(8,128)(2,1)}, u32[]{:S(2)}) copy-start(bf16[640,1024]{1,0:T(8,128)(2,1)} %param.10) | copy-start | bytes 3932164
  0.6 60.8 %copy-start.1 = (bf16[512,128]{1,0:T(8,128)(2,1)S(1)}, bf16[512,128]{1,0:T(8,128)(2,1)}, u32[]{:S(2)}) copy-start(bf16[512,128]{1,0:T(8,128)(2,1)} %param.9) | copy-start | bytes 393220
  0.7 61.0 %copy-start.2 = (bf16[512,640]{1,0:T(8,128)(2,1)S(1)}, bf16[512,640]{1,0:T(8,128)(2,1)}, u32[]{:S(2)}) copy-start(bf16[512,640]{1,0:T(8,128)(2,1)} %param.8) | copy-start | bytes 1966084
  2.4 37.0 %all-to-all-start = ((bf16[96,4,128]{2,1,0:T(4,128)(2,1)}), bf16[96,4,128]{2,1,0:T(4,128)(2,1)S(1)}, u32[]{:S(2)}, u32[]{:S(2)}) async-start(bf16[96,4,128]{2,1,0:T(4,128)(2,1)} %bitcast.35), calls=%async_computation | async-start | bytes 196608 | tf_op jit(solution)/shard_map/all_to_all | solution.py:84
  24.4 22.9 %collective-permute-start = (bf16[512,128]{1,0:T(8,128)(2,1)}, bf16[512,128]{1,0:T(8,128)(2,1)S(1)}, u32[]{:S(2)}, u32[]{:S(2)}) collective-permute-start(bf16[512,128]{1,0:T(8,128)(2,1)} %param.9), channel_id=1, source_target_pairs={{0,1},{1,0},{2,3},{3,2},{4,5},{5,4},{6,7},{7,6},{8,9},{9,8},{10,11... | collective-permute-start | bytes 393224 | tf_op jit(solution)/shard_map/ppermute | solution.py:77
  40.6 20.6 %all-to-all-start.1 = ((bf16[96,4,128]{2,1,0:T(4,128)(2,1)}), bf16[96,4,128]{2,1,0:T(4,128)(2,1)S(1)}, u32[]{:S(2)}, u32[]{:S(2)}) async-start(bf16[96,4,128]{2,1,0:T(4,128)(2,1)} %bitcast.3), calls=%async_computation.1 | async-start | bytes 196608 | tf_op jit(solution)/shard_map/all_to_all | solution.py:92
  48.3 19.4 %collective-permute-start.1 = (bf16[512,256]{1,0:T(8,128)(2,1)S(1)}, bf16[512,256]{1,0:T(8,128)(2,1)}, u32[]{:S(2)}, u32[]{:S(2)}) collective-permute-start(bf16[512,256]{1,0:T(8,128)(2,1)S(1)} %maximum_select_fusion.3), channel_id=1, source_target_pairs={{0,2},{1,3},{2,0},{3,1},{4,6},{5,7},{6,4},{7,5},{8,10},{9,11},{10,... | collective-permute-start | bytes 786440 | tf_op jit(solution)/shard_map/ppermute | solution.py:78
  62.7 10.9 %all-to-all-start.2 = ((bf16[8,4,32,128]{3,2,1,0:T(8,128)(2,1)}), bf16[8,4,32,128]{3,2,1,0:T(8,128)(2,1)S(1)}, u32[]{:S(2)}, u32[]{:S(2)}) async-start(bf16[8,4,32,128]{3,2,1,0:T(8,128)(2,1)} %broadcast_in_dim.4), calls=%async_computation.2 | async-start | bytes 524288 | tf_op jit(solution)/shard_map/all_to_all | solution.py:102
  68.9 22.5 %collective-permute-start.2 = (bf16[512,512]{1,0:T(8,128)(2,1)S(1)}, bf16[512,512]{1,0:T(8,128)(2,1)}, u32[]{:S(2)}, u32[]{:S(2)}) collective-permute-start(bf16[512,512]{1,0:T(8,128)(2,1)S(1)} %maximum_select_fusion.2), channel_id=1, source_target_pairs={{0,6},{1,7},{2,4},{3,5},{4,2},{5,3},{6,0},{7,1},{8,14},{9,15},{10,... | collective-permute-start | bytes 1572872 | tf_op jit(solution)/shard_map/ppermute | solution.py:79
  74.5 12.4 %all-to-all-start.3 = ((bf16[8,4,16,128]{3,1,2,0:T(4,128)(2,1)}), bf16[8,4,16,128]{3,1,2,0:T(4,128)(2,1)S(1)}, u32[]{:S(2)}, u32[]{:S(2)}) async-start(bf16[8,4,16,128]{3,1,2,0:T(4,128)(2,1)} %broadcast_in_dim.5), calls=%async_computation.3 | async-start | bytes 262144 | tf_op jit(solution)/shard_map/all_to_all | solution.py:111
  87.9 15.0 %all-to-all-start.4 = ((bf16[12,2,16,128]{3,1,2,0:T(2,128)(2,1)}), bf16[12,2,16,128]{3,1,2,0:T(2,128)(2,1)S(1)}, u32[]{:S(2)}, u32[]{:S(2)}) async-start(bf16[12,2,16,128]{3,1,2,0:T(2,128)(2,1)} %copy.37), calls=%async_computation.4 | async-start | bytes 196608 | tf_op jit(solution)/shard_map/all_to_all | solution.py:123

commit v4 on v3

--- a/solution.py
+++ b/solution.py
@@ -1,3 +1,5 @@
+import functools
+
 import jax
 import jax.numpy as jnp
 from jax import lax
@@ -7,6 +9,8 @@
 
 adapter_scale_factor = 2.0
 LINE = 8
+FIRST_Z = 9
+FIRST_Y = 4
 LANES = 128
 CORES = 2
 
@@ -14,7 +18,17 @@
 SPARE = 4
 
 
-def pack_kernel(adapter_ref, owner_ref, down_ref, up_ref, out_ref):
+def listed(z, y, columns):
+    return lax.rem(z + (columns - FIRST_Z), columns), lax.rem(y + (LINE - FIRST_Y), LINE)
+
+
+def listed_slot(slot, slots, columns):
+    owner = lax.div(slot, slots)
+    z, y = listed(lax.div(owner, LINE), lax.rem(owner, LINE), columns)
+    return (z * LINE + y) * slots + lax.rem(slot, slots)
+
+
+def pack_kernel(columns, adapter_ref, owner_ref, down_ref, up_ref, out_ref):
     slots, rank, dpiece = down_ref.shape
     blocks = adapter_ref.shape[0]
     rows = rank * SPARE
@@ -25,7 +39,7 @@
     lane = lax.broadcasted_iota(jnp.int32, (rows, LANES), 1)
     numbers = jnp.zeros((rows, LANES), jnp.float32)
     for b in range(blocks):
-        slot = owner_ref[adapter_ref[b]].astype(jnp.float32)
+        slot = listed_slot(owner_ref[adapter_ref[b]], slots, columns).astype(jnp.float32)
         numbers = jnp.where((kind == slots) & (lane == b), slot, numbers)
     down = jnp.concatenate([down_ref[j] for j in range(slots)], axis=0)
     up = jnp.concatenate([up_ref[j] for j in range(slots)], axis=0)
@@ -35,12 +49,12 @@
         out_ref[c * rows : (c + 1) * rows, :] = (mixed + numbers).astype(jnp.bfloat16)
 
 
-def pack(block_adapter, owner_map, down_rows, up_b):
+def pack(columns, block_adapter, owner_map, down_rows, up_b):
     _, rank, dpiece = down_rows.shape
     smem = pl.BlockSpec(memory_space=pltpu.SMEM)
     vmem = pl.BlockSpec(memory_space=pltpu.VMEM)
     return pl.pallas_call(
-        pack_kernel,
+        functools.partial(pack_kernel, columns),
         out_shape=jax.ShapeDtypeStruct((SPARE * rank * (dpiece // LANES + 1), LANES), jnp.bfloat16),
         in_specs=[smem, smem, vmem, vmem],
         out_specs=vmem,
@@ -59,10 +73,13 @@
     tensor = lax.axis_size("tensor")
     columns = dp // LINE
     chunks = dpiece // LANES
-    y_groups = [[z * LINE + y for y in range(LINE)] for z in range(columns)]
-    z_groups = [[z * LINE + y for z in range(columns)] for y in range(LINE)]
-    my_y = lax.axis_index("dp") % LINE
-    my_row = lax.axis_index("dp") // LINE
+    z_list = [(FIRST_Z + z) % columns for z in range(columns)]
+    y_list = [(FIRST_Y + y) % LINE for y in range(LINE)]
+    plane = [[z * LINE + y for z in z_list for y in y_list]]
+    y_groups = [[z * LINE + y for y in y_list] for z in range(columns)]
+    z_groups = [[z * LINE + y for z in z_list] for y in range(LINE)]
+    my_dp = lax.axis_index("dp")
+    my_row, my_y = listed(lax.div(my_dp, LINE), lax.rem(my_dp, LINE), columns)
 
     my_tensor = lax.axis_index("tensor")
     my_x, my_core = my_tensor // CORES, my_tensor % CORES
@@ -80,8 +97,10 @@
 
     live = (token_adapter >= 0).astype(jnp.float32)
 
-    pieces = pack(block_adapter, owner_map, down_a.transpose(0, 2, 1), up_b)
-    table = lax.all_to_all(pieces.reshape(dp, SPARE, LANES), "dp", 0, 0)
+    pieces = pack(columns, block_adapter, owner_map, down_a.transpose(0, 2, 1), up_b)
+    table = lax.all_to_all(
+        pieces.reshape(dp, SPARE, LANES), "dp", 0, 0, axis_index_groups=plane
+    )
     all_slots = table[:, own_slots, :block_count].astype(jnp.int32)
     table = table[:, :own_slots].reshape(dp * own_slots, LANES)
 
@@ -89,7 +108,9 @@
         all_slots.reshape(-1, 1) == jnp.arange(dp * own_slots, dtype=jnp.int32)[None, :]
     ).astype(jnp.bfloat16)
     picked = jnp.dot(onehot, table, preferred_element_type=jnp.float32).astype(jnp.bfloat16)
-    picked = lax.all_to_all(picked.reshape(dp, block_count, LANES), "dp", 0, 0)
+    picked = lax.all_to_all(
+        picked.reshape(dp, block_count, LANES), "dp", 0, 0, axis_index_groups=plane
+    )
     picked = picked.reshape(chunks + 1, rank, block_count, LANES)
     down_sel = picked[:chunks].transpose(2, 1, 0, 3).reshape(block_count, rank, dpiece)
     up_sel = picked[chunks].transpose(1, 0, 2)

time: 104 us -> 95.5 us (0.918)
  the two profiles are of different devices: /device:TPU:2 before, /device:TPU:8 now
where the time goes in v4:
time: 95.5 us; the launch traced here: 94.8 us
  starting transfers between devices  63.4 us (66%)
  waiting for transfers between devices  16.8 us (18%)
  matrix products  5.2 us (5%)
  other arithmetic  3.92 us (4%)
  local copies, waits for them, and re-layouts  2.78 us (3%)
  Pallas kernels  1.73 us (2%)
    all_to_all x1, starting transfers between devices, on_device(): lax.all_to_all(pieces.reshape(dp, SPARE, LANES), 'dp', 0, 0, axis_index_g...  22.3 us
    all_to_all x1, starting transfers between devices, on_device(): lax.all_to_all(picked.reshape(dp, block_count, LANES), 'dp', 0, 0, axis_i...  12 us
    all_to_all x1, starting transfers between devices, on_device(): lax.all_to_all(sums.astype(jnp.bfloat16).reshape(columns, own_slots, rank...  7.37 us
    all_to_all x1, starting transfers between devices, on_device(): lax.all_to_all(jnp.broadcast_to(terms, (LINE,) + terms.shape), 'dp', 0, 0...  7.03 us
    all_to_all x1, waiting for transfers between devices, on_device(): lax.all_to_all(pieces.reshape(dp, SPARE, LANES), 'dp', 0, 0, axis_index_g...  5.84 us
    ppermute x1, starting transfers between devices, on_device(): full_cotangent = both(held, lax.ppermute(held, 'tensor', far), my_x < 2)  5.14 us
    all_to_all x1, starting transfers between devices, on_device(): lax.all_to_all(jnp.broadcast_to(part, (tensor,) + part.shape), 'tensor',...  4.3 us
    all_to_all x1, waiting for transfers between devices, on_device(): lax.all_to_all(jnp.broadcast_to(terms, (LINE,) + terms.shape), 'dp', 0, 0...  3.87 us
  transfers between devices with their start and end apart: 8, of which 5 were waited for; matrix products, arithmetic and copies ran while one was open for 12% of the time, Pallas kernels for 0%

profile of v4, /device:TPU:8, one launch (start us, length us, event | category | flops | bytes accessed | tf_op | source)
XLA Modules:
  0.0 94.8 jit_solution(7085323485634680992)
XLA Ops:
  0.6 0.0 copy-start
  0.6 0.0 copy-start.1
  0.7 0.0 copy-start.2
  0.7 1.7 %shard_map.95 = bf16[384,128]{1,0:T(8,128)(2,1)} custom-call(s32[4]{0:T(128)} %adapter_ref.1, s32[192]{0:T(256)} %owner_ref.1, bf16[2,16,640]{2,1,0:T(8,128)(2,1)} %bitcast.39, bf16[2,16,128]{2,1,0:T(8,128)(2,1)} %up_ref.1), custom_call_target="tpu_custom_call" | custom-call | tf_op jit(solution)/shard_map/pallas_call | solution.py:56
  2.4 22.3 %all-to-all-start = ((bf16[96,4,128]{2,1,0:T(4,128)(2,1)}), bf16[96,4,128]{2,1,0:T(4,128)(2,1)S(1)}, u32[]{:S(2)}, u32[]{:S(2)}) async-start(bf16[96,4,128]{2,1,0:T(4,128)(2,1)} %bitcast.35), calls=%async_computation | async-start | bytes 196608 | tf_op jit(solution)/shard_map/all_to_all | solution.py:101
  24.7 1.9 %collective-permute-start = (bf16[512,128]{1,0:T(8,128)(2,1)}, bf16[512,128]{1,0:T(8,128)(2,1)S(1)}, u32[]{:S(2)}, u32[]{:S(2)}) collective-permute-start(bf16[512,128]{1,0:T(8,128)(2,1)} %param.9), channel_id=1, source_target_pairs={{0,1},{1,0},{2,3},{3,2},{4,5},{5,4},{6,7},{7,6},{8,9},{9,8},{10,11... | collective-permute-start | bytes 393224 | tf_op jit(solution)/shard_map/ppermute | solution.py:94
  26.7 0.1 iota_add_fusion
  26.7 0.1 add.60
  26.8 5.8 %all-to-all-done = bf16[96,4,128]{2,1,0:T(4,128)(2,1)S(1)} async-done(((bf16[96,4,128]{2,1,0:T(4,128)(2,1)}), bf16[96,4,128]{2,1,0:T(4,128)(2,1)S(1)}, u32[]{:S(2)}, u32[]{:S(2)}) %all-to-all-start) | async-done | bytes 98336 | tf_op jit(solution)/shard_map/all_to_all | solution.py:101
  32.7 0.2 fusion.18
  32.9 0.1 reshape.79
  33.0 0.9 convolution_convert_fusion.1
  33.9 12.0 %all-to-all-start.1 = ((bf16[96,4,128]{2,1,0:T(4,128)(2,1)}), bf16[96,4,128]{2,1,0:T(4,128)(2,1)S(1)}, u32[]{:S(2)}, u32[]{:S(2)}) async-start(bf16[96,4,128]{2,1,0:T(4,128)(2,1)} %bitcast.3), calls=%async_computation.1 | async-start | bytes 196608 | tf_op jit(solution)/shard_map/all_to_all | solution.py:111
  46.0 0.7 compare_convert_fusion
  46.6 0.0 collective-permute-done
  46.6 1.1 %maximum_select_fusion.3 = bf16[512,256]{1,0:T(8,128)(2,1)S(1)} fusion(bf16[512,128]{1,0:T(8,128)(2,1)S(1)} %collective-permute-done, bf16[512,128]{1,0:T(8,128)(2,1)} %param.9, pred[]{:T(512)S(6)} %eq.38), kind=kLoop, calls=%fused_computation.20 | loop fusion | flops 1179648 | bytes 524289 | tf_op jit(solution)/shard_map/jit(_where)/select_n | solution.py:89
  47.7 3.4 %collective-permute-start.1 = (bf16[512,256]{1,0:T(8,128)(2,1)S(1)}, bf16[512,256]{1,0:T(8,128)(2,1)}, u32[]{:S(2)}, u32[]{:S(2)}) collective-permute-start(bf16[512,256]{1,0:T(8,128)(2,1)S(1)} %maximum_select_fusion.3), channel_id=1, source_target_pairs={{0,2},{1,3},{2,0},{3,1},{4,6},{5,7},{6,4},{7,5},{8,10},{9,11},{10,... | collective-permute-start | bytes 786440 | tf_op jit(solution)/shard_map/ppermute | solution.py:95
  51.1 2.4 %all-to-all-done.1 = bf16[96,4,128]{2,1,0:T(4,128)(2,1)S(1)} async-done(((bf16[96,4,128]{2,1,0:T(4,128)(2,1)}), bf16[96,4,128]{2,1,0:T(4,128)(2,1)S(1)}, u32[]{:S(2)}, u32[]{:S(2)}) %all-to-all-start.1) | async-done | bytes 98336 | tf_op jit(solution)/shard_map/all_to_all | solution.py:111
  53.6 0.1 copy.47
  53.6 0.1 reshape.74
  53.8 0.0 copy-done.1
  53.8 0.2 convolution_convert_fusion.2
  54.0 0.0 copy-done.2
  54.0 0.3 convolution_convert_fusion.3
  54.3 0.8 broadcast_in_dim.4
  55.1 4.3 %all-to-all-start.2 = ((bf16[8,4,32,128]{3,2,1,0:T(8,128)(2,1)}), bf16[8,4,32,128]{3,2,1,0:T(8,128)(2,1)S(1)}, u32[]{:S(2)}, u32[]{:S(2)}) async-start(bf16[8,4,32,128]{3,2,1,0:T(8,128)(2,1)} %broadcast_in_dim.4), calls=%async_computation.2 | async-start | bytes 524288 | tf_op jit(solution)/shard_map/all_to_all | solution.py:123
  59.4 0.1 slice_convert_fusion
  59.5 0.1 eq.43
  59.5 0.0 collective-permute-done.1
  59.6 1.2 %maximum_select_fusion.2 = bf16[512,512]{1,0:T(8,128)(2,1)S(1)} fusion(bf16[512,256]{1,0:T(8,128)(2,1)} %collective-permute-done.1, bf16[512,256]{1,0:T(8,128)(2,1)S(1)} %maximum_select_fusion.3, pred[]{:T(512)S(6)} %eq.37), kind=kLoop, calls=%fused_computation.17 | loop fusion | flops 2359296 | bytes 1048577 | tf_op jit(solution)/shard_map/jit(_where)/select_n | solution.py:89
  60.7 5.1 %collective-permute-start.2 = (bf16[512,512]{1,0:T(8,128)(2,1)S(1)}, bf16[512,512]{1,0:T(8,128)(2,1)}, u32[]{:S(2)}, u32[]{:S(2)}) collective-permute-start(bf16[512,512]{1,0:T(8,128)(2,1)S(1)} %maximum_select_fusion.2), channel_id=1, source_target_pairs={{0,6},{1,7},{2,4},{3,5},{4,2},{5,3},{6,0},{7,1},{8,14},{9,15},{10,... | collective-permute-start | bytes 1572872 | tf_op jit(solution)/shard_map/ppermute | solution.py:96
  65.9 1.0 %all-to-all-done.2 = bf16[8,4,32,128]{3,2,1,0:T(8,128)(2,1)S(1)} async-done(((bf16[8,4,32,128]{3,2,1,0:T(8,128)(2,1)}), bf16[8,4,32,128]{3,2,1,0:T(8,128)(2,1)S(1)}, u32[]{:S(2)}, u32[]{:S(2)}) %all-to-all-start.2) | async-done | bytes 262176 | tf_op jit(solution)/shard_map/all_to_all | solution.py:123
  66.9 0.1 fusion.2
  67.1 0.7 broadcast_in_dim.5
  67.8 7.0 %all-to-all-start.3 = ((bf16[8,4,16,128]{3,1,2,0:T(4,128)(2,1)}), bf16[8,4,16,128]{3,1,2,0:T(4,128)(2,1)S(1)}, u32[]{:S(2)}, u32[]{:S(2)}) async-start(bf16[8,4,16,128]{3,1,2,0:T(4,128)(2,1)} %broadcast_in_dim.5), calls=%async_computation.3 | async-start | bytes 262144 | tf_op jit(solution)/shard_map/all_to_all | solution.py:132
  74.8 0.4 convolution_multiply_fusion.1
  75.2 3.9 %all-to-all-done.3 = bf16[8,4,16,128]{3,1,2,0:T(4,128)(2,1)S(1)} async-done(((bf16[8,4,16,128]{3,1,2,0:T(4,128)(2,1)}), bf16[8,4,16,128]{3,1,2,0:T(4,128)(2,1)S(1)}, u32[]{:S(2)}, u32[]{:S(2)}) %all-to-all-start.3) | async-done | bytes 131104 | tf_op jit(solution)/shard_map/all_to_all | solution.py:132
  79.1 0.2 convolution_convert_fusion
  79.4 0.7 copy.37
  80.1 7.4 %all-to-all-start.4 = ((bf16[12,2,16,128]{3,1,2,0:T(2,128)(2,1)}), bf16[12,2,16,128]{3,1,2,0:T(2,128)(2,1)S(1)}, u32[]{:S(2)}, u32[]{:S(2)}) async-start(bf16[12,2,16,128]{3,1,2,0:T(2,128)(2,1)} %copy.37), calls=%async_computation.4 | async-start | bytes 196608 | tf_op jit(solution)/shard_map/all_to_all | solution.py:144
  87.4 0.0 collective-permute-done.2
  87.4 0.0 copy-done
  87.5 3.1 %fusion.1 = bf16[512,640]{1,0:T(8,128)(2,1)} fusion(f32[512,640]{1,0:T(8,128)S(1)} %bitcast.29, bf16[640,1024]{1,0:T(8,128)(2,1)S(1)} %copy-done, bf16[512,512]{1,0:T(8,128)(2,1)} %collective-permute-done.2, bf16[512,512]{1,0:T(8,128)(2,1)S(1)} %maximum_select_fusion.2, pred[]{:T(512)S(6)} %lt.16, f32[512]{0:T(512)S(1)} %get-tuple-element.8), kind=kOutput, calls=%fused_computation.3 | convolution fusion | flops 676790272 | bytes 4327425 | tf_op jit(solution)/shard_map/dot_general | solution.py:149
  90.5 3.7 %all-to-all-done.4 = bf16[12,2,16,128]{3,1,2,0:T(2,128)(2,1)S(1)} async-done(((bf16[12,2,16,128]{3,1,2,0:T(2,128)(2,1)}), bf16[12,2,16,128]{3,1,2,0:T(2,128)(2,1)S(1)}, u32[]{:S(2)}, u32[]{:S(2)}) %all-to-all-start.4) | async-done | bytes 98336 | tf_op jit(solution)/shard_map/all_to_all | solution.py:144
  94.2 0.6 convert_reduce_fusion.1
  (10 shorter events, 0.2 us)
Async XLA Ops:
  0.6 86.8 %copy-start = (bf16[640,1024]{1,0:T(8,128)(2,1)S(1)}, bf16[640,1024]{1,0:T(8,128)(2,1)}, u32[]{:S(2)}) copy-start(bf16[640,1024]{1,0:T(8,128)(2,1)} %param.10) | copy-start | bytes 3932164
  0.6 53.1 %copy-start.1 = (bf16[512,128]{1,0:T(8,128)(2,1)S(1)}, bf16[512,128]{1,0:T(8,128)(2,1)}, u32[]{:S(2)}) copy-start(bf16[512,128]{1,0:T(8,128)(2,1)} %param.9) | copy-start | bytes 393220
  0.7 53.3 %copy-start.2 = (bf16[512,640]{1,0:T(8,128)(2,1)S(1)}, bf16[512,640]{1,0:T(8,128)(2,1)}, u32[]{:S(2)}) copy-start(bf16[512,640]{1,0:T(8,128)(2,1)} %param.8) | copy-start | bytes 1966084
  2.4 30.3 %all-to-all-start = ((bf16[96,4,128]{2,1,0:T(4,128)(2,1)}), bf16[96,4,128]{2,1,0:T(4,128)(2,1)S(1)}, u32[]{:S(2)}, u32[]{:S(2)}) async-start(bf16[96,4,128]{2,1,0:T(4,128)(2,1)} %bitcast.35), calls=%async_computation | async-start | bytes 196608 | tf_op jit(solution)/shard_map/all_to_all | solution.py:101
  24.7 22.0 %collective-permute-start = (bf16[512,128]{1,0:T(8,128)(2,1)}, bf16[512,128]{1,0:T(8,128)(2,1)S(1)}, u32[]{:S(2)}, u32[]{:S(2)}) collective-permute-start(bf16[512,128]{1,0:T(8,128)(2,1)} %param.9), channel_id=1, source_target_pairs={{0,1},{1,0},{2,3},{3,2},{4,5},{5,4},{6,7},{7,6},{8,9},{9,8},{10,11... | collective-permute-start | bytes 393224 | tf_op jit(solution)/shard_map/ppermute | solution.py:94
  33.9 19.6 %all-to-all-start.1 = ((bf16[96,4,128]{2,1,0:T(4,128)(2,1)}), bf16[96,4,128]{2,1,0:T(4,128)(2,1)S(1)}, u32[]{:S(2)}, u32[]{:S(2)}) async-start(bf16[96,4,128]{2,1,0:T(4,128)(2,1)} %bitcast.3), calls=%async_computation.1 | async-start | bytes 196608 | tf_op jit(solution)/shard_map/all_to_all | solution.py:111
  47.7 11.9 %collective-permute-start.1 = (bf16[512,256]{1,0:T(8,128)(2,1)S(1)}, bf16[512,256]{1,0:T(8,128)(2,1)}, u32[]{:S(2)}, u32[]{:S(2)}) collective-permute-start(bf16[512,256]{1,0:T(8,128)(2,1)S(1)} %maximum_select_fusion.3), channel_id=1, source_target_pairs={{0,2},{1,3},{2,0},{3,1},{4,6},{5,7},{6,4},{7,5},{8,10},{9,11},{10,... | collective-permute-start | bytes 786440 | tf_op jit(solution)/shard_map/ppermute | solution.py:95
  55.1 11.8 %all-to-all-start.2 = ((bf16[8,4,32,128]{3,2,1,0:T(8,128)(2,1)}), bf16[8,4,32,128]{3,2,1,0:T(8,128)(2,1)S(1)}, u32[]{:S(2)}, u32[]{:S(2)}) async-start(bf16[8,4,32,128]{3,2,1,0:T(8,128)(2,1)} %broadcast_in_dim.4), calls=%async_computation.2 | async-start | bytes 524288 | tf_op jit(solution)/shard_map/all_to_all | solution.py:123
  60.7 26.7 %collective-permute-start.2 = (bf16[512,512]{1,0:T(8,128)(2,1)S(1)}, bf16[512,512]{1,0:T(8,128)(2,1)}, u32[]{:S(2)}, u32[]{:S(2)}) collective-permute-start(bf16[512,512]{1,0:T(8,128)(2,1)S(1)} %maximum_select_fusion.2), channel_id=1, source_target_pairs={{0,6},{1,7},{2,4},{3,5},{4,2},{5,3},{6,0},{7,1},{8,14},{9,15},{10,... | collective-permute-start | bytes 1572872 | tf_op jit(solution)/shard_map/ppermute | solution.py:96
  67.8 11.3 %all-to-all-start.3 = ((bf16[8,4,16,128]{3,1,2,0:T(4,128)(2,1)}), bf16[8,4,16,128]{3,1,2,0:T(4,128)(2,1)S(1)}, u32[]{:S(2)}, u32[]{:S(2)}) async-start(bf16[8,4,16,128]{3,1,2,0:T(4,128)(2,1)} %broadcast_in_dim.5), calls=%async_computation.3 | async-start | bytes 262144 | tf_op jit(solution)/shard_map/all_to_all | solution.py:132
  80.1 14.1 %all-to-all-start.4 = ((bf16[12,2,16,128]{3,1,2,0:T(2,128)(2,1)}), bf16[12,2,16,128]{3,1,2,0:T(2,128)(2,1)S(1)}, u32[]{:S(2)}, u32[]{:S(2)}) async-start(bf16[12,2,16,128]{3,1,2,0:T(2,128)(2,1)} %copy.37), calls=%async_computation.4 | async-start | bytes 196608 | tf_op jit(solution)/shard_map/all_to_all | solution.py:144

commit v5 on v4

--- a/solution.py
+++ b/solution.py
@@ -11,6 +11,8 @@
 LINE = 8
 FIRST_Z = 9
 FIRST_Y = 4
+LAST_Z = 7
+FIRST_X = 2
 LANES = 128
 CORES = 2
 
@@ -18,8 +20,22 @@
 SPARE = 4
 
 
+def far_first(at, first, extent):
+    past = lax.rem(at + (extent - first), extent) - extent // 2
+    return lax.select(past >= 0, 2 * past + 1, lax.rem(-2 * past, extent))
+
+
+def far_first_list(first, extent):
+    aside = [first]
+    for step in range(extent - 1):
+        past = (step + 1) // 2
+        past = past if step % 2 == 0 else -past
+        aside.append((first + extent // 2 + past) % extent)
+    return aside
+
+
 def listed(z, y, columns):
-    return lax.rem(z + (columns - FIRST_Z), columns), lax.rem(y + (LINE - FIRST_Y), LINE)
+    return far_first(z, FIRST_Z, columns), far_first(y, FIRST_Y, LINE)
 
 
 def listed_slot(slot, slots, columns):
@@ -73,11 +89,14 @@
     tensor = lax.axis_size("tensor")
     columns = dp // LINE
     chunks = dpiece // LANES
-    z_list = [(FIRST_Z + z) % columns for z in range(columns)]
-    y_list = [(FIRST_Y + y) % LINE for y in range(LINE)]
+    z_list = far_first_list(FIRST_Z, columns)
+    y_list = far_first_list(FIRST_Y, LINE)
     plane = [[z * LINE + y for z in z_list for y in y_list]]
     y_groups = [[z * LINE + y for y in y_list] for z in range(columns)]
-    z_groups = [[z * LINE + y for z in z_list] for y in range(LINE)]
+    last_list = far_first_list(LAST_Z, columns)
+    z_groups = [[z * LINE + y for z in last_list] for y in range(LINE)]
+    x_list = far_first_list(FIRST_X, tensor // CORES)
+    t_group = [[x * CORES + core for x in x_list for core in reversed(range(CORES))]]
     my_dp = lax.axis_index("dp")
     my_row, my_y = listed(lax.div(my_dp, LINE), lax.rem(my_dp, LINE), columns)
 
@@ -120,7 +139,9 @@
     low_part = jnp.einsum("brd,bnd->brn", down_sel, input_blocks, preferred_element_type=jnp.float32)
     hid_part = jnp.einsum("brk,bnk->brn", up_sel, g_blocks, preferred_element_type=jnp.float32)
     part = jnp.concatenate([low_part, hid_part], axis=1).astype(jnp.bfloat16)
-    part = lax.all_to_all(jnp.broadcast_to(part, (tensor,) + part.shape), "tensor", 0, 0)
+    part = lax.all_to_all(
+        jnp.broadcast_to(part, (tensor,) + part.shape), "tensor", 0, 0, axis_index_groups=t_group
+    )
     total = jnp.sum(part.astype(jnp.float32), axis=0) * live.reshape(block_count, 1, blk_rows)
     total = total.astype(jnp.bfloat16)
     low_rank, hidden = total[:, :rank], total[:, rank:]
@@ -135,7 +156,7 @@
     terms = terms.reshape(LINE * block_count, rank, kpiece)
     row_slots = lax.dynamic_slice_in_dim(all_slots, my_row * LINE, LINE, 0).reshape(-1)
     column_slots = (
-        jnp.arange(columns, dtype=jnp.int32)[:, None] * (LINE * own_slots)
+        jnp.array([z_list.index(z) for z in last_list], jnp.int32)[:, None] * (LINE * own_slots)
         + my_y * own_slots
         + jnp.arange(own_slots, dtype=jnp.int32)[None, :]
     ).reshape(-1)

time: 95.5 us -> 93.1 us (0.975)
  the two profiles are of different devices: /device:TPU:8 before, /device:TPU:4 now
where the time goes in v5:
time: 93.1 us; the launch traced here: 92.4 us
  starting transfers between devices  65.8 us (71%)
  waiting for transfers between devices  11.4 us (12%)
  matrix products  5.19 us (6%)
  other arithmetic  4.58 us (5%)
  local copies, waits for them, and re-layouts  2.78 us (3%)
  Pallas kernels  1.73 us (2%)
    all_to_all x1, starting transfers between devices, on_device(): lax.all_to_all(pieces.reshape(dp, SPARE, LANES), 'dp', 0, 0, axis_index_g...  23.4 us
    all_to_all x1, starting transfers between devices, on_device(): lax.all_to_all(picked.reshape(dp, block_count, LANES), 'dp', 0, 0, axis_i...  13.1 us
    all_to_all x1, starting transfers between devices, on_device(): lax.all_to_all(sums.astype(jnp.bfloat16).reshape(columns, own_slots, rank...  9.8 us
    all_to_all x1, starting transfers between devices, on_device(): lax.all_to_all(jnp.broadcast_to(terms, (LINE,) + terms.shape), 'dp', 0, 0...  8.37 us
    all_to_all x1, waiting for transfers between devices, on_device(): lax.all_to_all(jnp.broadcast_to(terms, (LINE,) + terms.shape), 'dp', 0, 0...  4.05 us
    all_to_all x1, waiting for transfers between devices, on_device(): lax.all_to_all(pieces.reshape(dp, SPARE, LANES), 'dp', 0, 0, axis_index_g...  3.87 us
    all_to_all x1, starting transfers between devices, on_device(): lax.all_to_all(jnp.broadcast_to(part, (tensor,) + part.shape), 'tensor',...  3.36 us
    ppermute x1, starting transfers between devices, on_device(): held = both(held, lax.ppermute(held, 'tensor', pair), my_x % 2 == 0)  3.11 us
  transfers between devices with their start and end apart: 8, of which 5 were waited for; matrix products, arithmetic and copies ran while one was open for 13% of the time, Pallas kernels for 0%

profile of v5, /device:TPU:4, one launch (start us, length us, event | category | flops | bytes accessed | tf_op | source)
XLA Modules:
  0.0 92.4 jit_solution(4237610171782788007)
XLA Ops:
  0.6 0.0 copy-start
  0.6 0.0 copy-start.1
  0.7 0.0 copy-start.2
  0.7 1.7 %shard_map.104 = bf16[384,128]{1,0:T(8,128)(2,1)} custom-call(s32[4]{0:T(128)} %adapter_ref.1, s32[192]{0:T(256)} %owner_ref.1, bf16[2,16,640]{2,1,0:T(8,128)(2,1)} %bitcast.39, bf16[2,16,128]{2,1,0:T(8,128)(2,1)} %up_ref.1), custom_call_target="tpu_custom_call" | custom-call | tf_op jit(solution)/shard_map/pallas_call | solution.py:72
  2.4 23.4 %all-to-all-start = ((bf16[96,4,128]{2,1,0:T(4,128)(2,1)}), bf16[96,4,128]{2,1,0:T(4,128)(2,1)S(1)}, u32[]{:S(2)}, u32[]{:S(2)}) async-start(bf16[96,4,128]{2,1,0:T(4,128)(2,1)} %bitcast.35), calls=%async_computation | async-start | bytes 196608 | tf_op jit(solution)/shard_map/all_to_all | solution.py:120
  25.8 1.9 %collective-permute-start = (bf16[512,128]{1,0:T(8,128)(2,1)}, bf16[512,128]{1,0:T(8,128)(2,1)S(1)}, u32[]{:S(2)}, u32[]{:S(2)}) collective-permute-start(bf16[512,128]{1,0:T(8,128)(2,1)} %param.10), channel_id=1, source_target_pairs={{0,1},{1,0},{2,3},{3,2},{4,5},{5,4},{6,7},{7,6},{8,9},{9,8},{10,11... | collective-permute-start | bytes 393224 | tf_op jit(solution)/shard_map/ppermute | solution.py:113
  27.8 0.7 broadcast_add_fusion
  28.4 0.1 iota_add_fusion
  28.5 0.1 add.65
  28.6 3.9 %all-to-all-done = bf16[96,4,128]{2,1,0:T(4,128)(2,1)S(1)} async-done(((bf16[96,4,128]{2,1,0:T(4,128)(2,1)}), bf16[96,4,128]{2,1,0:T(4,128)(2,1)S(1)}, u32[]{:S(2)}, u32[]{:S(2)}) %all-to-all-start) | async-done | bytes 98336 | tf_op jit(solution)/shard_map/all_to_all | solution.py:120
  32.5 0.2 fusion.18
  32.7 0.1 reshape.75
  32.8 0.9 convolution_convert_fusion.1
  33.7 13.1 %all-to-all-start.1 = ((bf16[96,4,128]{2,1,0:T(4,128)(2,1)}), bf16[96,4,128]{2,1,0:T(4,128)(2,1)S(1)}, u32[]{:S(2)}, u32[]{:S(2)}) async-start(bf16[96,4,128]{2,1,0:T(4,128)(2,1)} %bitcast.3), calls=%async_computation.1 | async-start | bytes 196608 | tf_op jit(solution)/shard_map/all_to_all | solution.py:130
  46.8 0.7 compare_convert_fusion
  47.5 0.0 collective-permute-done
  47.5 1.1 %maximum_select_fusion.3 = bf16[512,256]{1,0:T(8,128)(2,1)S(1)} fusion(bf16[512,128]{1,0:T(8,128)(2,1)S(1)} %collective-permute-done, bf16[512,128]{1,0:T(8,128)(2,1)} %param.10, pred[]{:T(512)S(6)} %eq.38), kind=kLoop, calls=%fused_computation.20 | loop fusion | flops 1179648 | bytes 524289 | tf_op jit(solution)/shard_map/jit(_where)/select_n | solution.py:108
  48.6 3.1 %collective-permute-start.1 = (bf16[512,256]{1,0:T(8,128)(2,1)S(1)}, bf16[512,256]{1,0:T(8,128)(2,1)}, u32[]{:S(2)}, u32[]{:S(2)}) collective-permute-start(bf16[512,256]{1,0:T(8,128)(2,1)S(1)} %maximum_select_fusion.3), channel_id=1, source_target_pairs={{0,2},{1,3},{2,0},{3,1},{4,6},{5,7},{6,4},{7,5},{8,10},{9,11},{10,... | collective-permute-start | bytes 786440 | tf_op jit(solution)/shard_map/ppermute | solution.py:114
  51.7 1.3 %all-to-all-done.1 = bf16[96,4,128]{2,1,0:T(4,128)(2,1)S(1)} async-done(((bf16[96,4,128]{2,1,0:T(4,128)(2,1)}), bf16[96,4,128]{2,1,0:T(4,128)(2,1)S(1)}, u32[]{:S(2)}, u32[]{:S(2)}) %all-to-all-start.1) | async-done | bytes 98336 | tf_op jit(solution)/shard_map/all_to_all | solution.py:130
  53.0 0.1 copy.48
  53.1 0.1 reshape.70
  53.2 0.0 copy-done.1
  53.3 0.2 convolution_convert_fusion.2
  53.4 0.0 copy-done.2
  53.4 0.3 convolution_convert_fusion.3
  53.8 0.8 broadcast_in_dim.4
  54.5 3.4 %all-to-all-start.2 = ((bf16[8,4,32,128]{3,2,1,0:T(8,128)(2,1)}), bf16[8,4,32,128]{3,2,1,0:T(8,128)(2,1)S(1)}, u32[]{:S(2)}, u32[]{:S(2)}) async-start(bf16[8,4,32,128]{3,2,1,0:T(8,128)(2,1)} %broadcast_in_dim.4), calls=%async_computation.2 | async-start | bytes 524288 | tf_op jit(solution)/shard_map/all_to_all | solution.py:142
  57.9 0.1 slice_convert_fusion
  58.0 0.1 eq.43
  58.1 0.0 collective-permute-done.1
  58.1 1.2 %maximum_select_fusion.2 = bf16[512,512]{1,0:T(8,128)(2,1)S(1)} fusion(bf16[512,256]{1,0:T(8,128)(2,1)} %collective-permute-done.1, bf16[512,256]{1,0:T(8,128)(2,1)S(1)} %maximum_select_fusion.3, pred[]{:T(512)S(6)} %eq.37), kind=kLoop, calls=%fused_computation.17 | loop fusion | flops 2359296 | bytes 1048577 | tf_op jit(solution)/shard_map/jit(_where)/select_n | solution.py:108
  59.3 2.8 %collective-permute-start.2 = (bf16[512,512]{1,0:T(8,128)(2,1)S(1)}, bf16[512,512]{1,0:T(8,128)(2,1)}, u32[]{:S(2)}, u32[]{:S(2)}) collective-permute-start(bf16[512,512]{1,0:T(8,128)(2,1)S(1)} %maximum_select_fusion.2), channel_id=1, source_target_pairs={{0,6},{1,7},{2,4},{3,5},{4,2},{5,3},{6,0},{7,1},{8,14},{9,15},{10,... | collective-permute-start | bytes 1572872 | tf_op jit(solution)/shard_map/ppermute | solution.py:115
  62.1 1.3 %all-to-all-done.2 = bf16[8,4,32,128]{3,2,1,0:T(8,128)(2,1)S(1)} async-done(((bf16[8,4,32,128]{3,2,1,0:T(8,128)(2,1)}), bf16[8,4,32,128]{3,2,1,0:T(8,128)(2,1)S(1)}, u32[]{:S(2)}, u32[]{:S(2)}) %all-to-all-start.2) | async-done | bytes 262176 | tf_op jit(solution)/shard_map/all_to_all | solution.py:142
  63.4 0.1 fusion.2
  63.6 0.7 broadcast_in_dim.5
  64.3 8.4 %all-to-all-start.3 = ((bf16[8,4,16,128]{3,1,2,0:T(4,128)(2,1)}), bf16[8,4,16,128]{3,1,2,0:T(4,128)(2,1)S(1)}, u32[]{:S(2)}, u32[]{:S(2)}) async-start(bf16[8,4,16,128]{3,1,2,0:T(4,128)(2,1)} %broadcast_in_dim.5), calls=%async_computation.3 | async-start | bytes 262144 | tf_op jit(solution)/shard_map/all_to_all | solution.py:153
  72.7 0.4 convolution_multiply_fusion.1
  73.0 4.1 %all-to-all-done.3 = bf16[8,4,16,128]{3,1,2,0:T(4,128)(2,1)S(1)} async-done(((bf16[8,4,16,128]{3,1,2,0:T(4,128)(2,1)}), bf16[8,4,16,128]{3,1,2,0:T(4,128)(2,1)S(1)}, u32[]{:S(2)}, u32[]{:S(2)}) %all-to-all-start.3) | async-done | bytes 131104 | tf_op jit(solution)/shard_map/all_to_all | solution.py:153
  77.1 0.2 convolution_convert_fusion
  77.4 0.7 copy.38
  78.1 9.8 %all-to-all-start.4 = ((bf16[12,2,16,128]{3,1,2,0:T(2,128)(2,1)}), bf16[12,2,16,128]{3,1,2,0:T(2,128)(2,1)S(1)}, u32[]{:S(2)}, u32[]{:S(2)}) async-start(bf16[12,2,16,128]{3,1,2,0:T(2,128)(2,1)} %copy.38), calls=%async_computation.4 | async-start | bytes 196608 | tf_op jit(solution)/shard_map/all_to_all | solution.py:165
  87.9 0.0 collective-permute-done.2
  87.9 0.0 copy-done
  87.9 3.1 %fusion.1 = bf16[512,640]{1,0:T(8,128)(2,1)} fusion(f32[512,640]{1,0:T(8,128)S(1)} %bitcast.29, bf16[640,1024]{1,0:T(8,128)(2,1)S(1)} %copy-done, bf16[512,512]{1,0:T(8,128)(2,1)} %collective-permute-done.2, bf16[512,512]{1,0:T(8,128)(2,1)S(1)} %maximum_select_fusion.2, pred[]{:T(512)S(6)} %lt.16, f32[512]{0:T(512)S(1)} %get-tuple-element.8), kind=kOutput, calls=%fused_computation.3 | convolution fusion | flops 676790272 | bytes 4327425 | tf_op jit(solution)/shard_map/dot_general | solution.py:170
  90.9 0.8 all-to-all-done.4
  91.8 0.6 convert_reduce_fusion.1
  (9 shorter events, 0.2 us)
Async XLA Ops:
  0.6 87.2 %copy-start = (bf16[640,1024]{1,0:T(8,128)(2,1)S(1)}, bf16[640,1024]{1,0:T(8,128)(2,1)}, u32[]{:S(2)}) copy-start(bf16[640,1024]{1,0:T(8,128)(2,1)} %param.11) | copy-start | bytes 3932164
  0.6 52.6 %copy-start.1 = (bf16[512,128]{1,0:T(8,128)(2,1)S(1)}, bf16[512,128]{1,0:T(8,128)(2,1)}, u32[]{:S(2)}) copy-start(bf16[512,128]{1,0:T(8,128)(2,1)} %param.10) | copy-start | bytes 393220
  0.7 52.8 %copy-start.2 = (bf16[512,640]{1,0:T(8,128)(2,1)S(1)}, bf16[512,640]{1,0:T(8,128)(2,1)}, u32[]{:S(2)}) copy-start(bf16[512,640]{1,0:T(8,128)(2,1)} %param.9) | copy-start | bytes 1966084
  2.4 30.1 %all-to-all-start = ((bf16[96,4,128]{2,1,0:T(4,128)(2,1)}), bf16[96,4,128]{2,1,0:T(4,128)(2,1)S(1)}, u32[]{:S(2)}, u32[]{:S(2)}) async-start(bf16[96,4,128]{2,1,0:T(4,128)(2,1)} %bitcast.35), calls=%async_computation | async-start | bytes 196608 | tf_op jit(solution)/shard_map/all_to_all | solution.py:120
  25.8 21.7 %collective-permute-start = (bf16[512,128]{1,0:T(8,128)(2,1)}, bf16[512,128]{1,0:T(8,128)(2,1)S(1)}, u32[]{:S(2)}, u32[]{:S(2)}) collective-permute-start(bf16[512,128]{1,0:T(8,128)(2,1)} %param.10), channel_id=1, source_target_pairs={{0,1},{1,0},{2,3},{3,2},{4,5},{5,4},{6,7},{7,6},{8,9},{9,8},{10,11... | collective-permute-start | bytes 393224 | tf_op jit(solution)/shard_map/ppermute | solution.py:113
  33.7 19.3 %all-to-all-start.1 = ((bf16[96,4,128]{2,1,0:T(4,128)(2,1)}), bf16[96,4,128]{2,1,0:T(4,128)(2,1)S(1)}, u32[]{:S(2)}, u32[]{:S(2)}) async-start(bf16[96,4,128]{2,1,0:T(4,128)(2,1)} %bitcast.3), calls=%async_computation.1 | async-start | bytes 196608 | tf_op jit(solution)/shard_map/all_to_all | solution.py:130
  48.6 9.5 %collective-permute-start.1 = (bf16[512,256]{1,0:T(8,128)(2,1)S(1)}, bf16[512,256]{1,0:T(8,128)(2,1)}, u32[]{:S(2)}, u32[]{:S(2)}) collective-permute-start(bf16[512,256]{1,0:T(8,128)(2,1)S(1)} %maximum_select_fusion.3), channel_id=1, source_target_pairs={{0,2},{1,3},{2,0},{3,1},{4,6},{5,7},{6,4},{7,5},{8,10},{9,11},{10,... | collective-permute-start | bytes 786440 | tf_op jit(solution)/shard_map/ppermute | solution.py:114
  54.5 8.8 %all-to-all-start.2 = ((bf16[8,4,32,128]{3,2,1,0:T(8,128)(2,1)}), bf16[8,4,32,128]{3,2,1,0:T(8,128)(2,1)S(1)}, u32[]{:S(2)}, u32[]{:S(2)}) async-start(bf16[8,4,32,128]{3,2,1,0:T(8,128)(2,1)} %broadcast_in_dim.4), calls=%async_computation.2 | async-start | bytes 524288 | tf_op jit(solution)/shard_map/all_to_all | solution.py:142
  59.3 28.6 %collective-permute-start.2 = (bf16[512,512]{1,0:T(8,128)(2,1)S(1)}, bf16[512,512]{1,0:T(8,128)(2,1)}, u32[]{:S(2)}, u32[]{:S(2)}) collective-permute-start(bf16[512,512]{1,0:T(8,128)(2,1)S(1)} %maximum_select_fusion.2), channel_id=1, source_target_pairs={{0,6},{1,7},{2,4},{3,5},{4,2},{5,3},{6,0},{7,1},{8,14},{9,15},{10,... | collective-permute-start | bytes 1572872 | tf_op jit(solution)/shard_map/ppermute | solution.py:115
  64.3 12.8 %all-to-all-start.3 = ((bf16[8,4,16,128]{3,1,2,0:T(4,128)(2,1)}), bf16[8,4,16,128]{3,1,2,0:T(4,128)(2,1)S(1)}, u32[]{:S(2)}, u32[]{:S(2)}) async-start(bf16[8,4,16,128]{3,1,2,0:T(4,128)(2,1)} %broadcast_in_dim.5), calls=%async_computation.3 | async-start | bytes 262144 | tf_op jit(solution)/shard_map/all_to_all | solution.py:153
  78.1 13.7 %all-to-all-start.4 = ((bf16[12,2,16,128]{3,1,2,0:T(2,128)(2,1)}), bf16[12,2,16,128]{3,1,2,0:T(2,128)(2,1)S(1)}, u32[]{:S(2)}, u32[]{:S(2)}) async-start(bf16[12,2,16,128]{3,1,2,0:T(2,128)(2,1)} %copy.38), calls=%async_computation.4 | async-start | bytes 196608 | tf_op jit(solution)/shard_map/all_to_all | solution.py:165

commit v6 on v5

--- a/solution.py
+++ b/solution.py
@@ -112,7 +112,7 @@
     far = [(i, (last - i) ^ 1) for i in range(tensor)]
     held = both(cotangent, lax.ppermute(cotangent, "tensor", near), my_core == 0)
     held = both(held, lax.ppermute(held, "tensor", pair), my_x % 2 == 0)
-    full_cotangent = both(held, lax.ppermute(held, "tensor", far), my_x < 2)
+    swapped = lax.ppermute(held, "tensor", far)
 
     live = (token_adapter >= 0).astype(jnp.float32)
 
@@ -127,6 +127,11 @@
         all_slots.reshape(-1, 1) == jnp.arange(dp * own_slots, dtype=jnp.int32)[None, :]
     ).astype(jnp.bfloat16)
     picked = jnp.dot(onehot, table, preferred_element_type=jnp.float32).astype(jnp.bfloat16)
+    picked, late_weight = lax.optimization_barrier((picked, base_weight))
+    low_weight, high_weight = jnp.split(late_weight, 2, axis=1)
+    held_weight = jnp.where(my_x < 2, low_weight, high_weight)
+    swapped_weight = jnp.where(my_x < 2, high_weight, low_weight)
+    held_weight, swapped_weight = lax.optimization_barrier((held_weight, swapped_weight))
     picked = lax.all_to_all(
         picked.reshape(dp, block_count, LANES), "dp", 0, 0, axis_index_groups=plane
     )
@@ -150,6 +155,7 @@
         "brn,bno->bro", low_rank, g_blocks, preferred_element_type=jnp.float32
     )
     terms = terms.astype(jnp.bfloat16)
+    terms, hidden = lax.optimization_barrier((terms, hidden))
     terms = lax.all_to_all(
         jnp.broadcast_to(terms, (LINE,) + terms.shape), "dp", 0, 0, axis_index_groups=y_groups
     )
@@ -167,13 +173,16 @@
     )
     grad_b = jnp.sum(sums.astype(jnp.float32), axis=0)
 
-    frozen = lax.dot_general(
-        full_cotangent, base_weight, (((1,), (1,)), ((), ())), preferred_element_type=jnp.float32
-    )
+    contract_last = (((1,), (1,)), ((), ()))
     adapter = jnp.einsum(
         "brn,brd->bnd", hidden, down_sel, preferred_element_type=jnp.float32
     ).reshape(row_count, dpiece)
-    gradient = (frozen * live[:, None] + adapter_scale_factor * adapter).astype(jnp.bfloat16)
+    frozen = lax.dot_general(held, held_weight, contract_last, preferred_element_type=jnp.float32)
+    early = lax.optimization_barrier(frozen * live[:, None] + adapter_scale_factor * adapter)
+    frozen = lax.dot_general(
+        swapped, swapped_weight, contract_last, preferred_element_type=jnp.float32
+    )
+    gradient = (early + frozen * live[:, None]).astype(jnp.bfloat16)
     return (gradient, grad_b)
 
 

time: 93.1 us -> 93.4 us (level)
  the two profiles are of different devices: /device:TPU:4 before, /device:TPU:2 now
where the time goes in v6:
time: 93.4 us; the launch traced here: 92.5 us
  starting transfers between devices  65.5 us (70%)
  waiting for transfers between devices  9.62 us (10%)
  matrix products  6.45 us (7%)
  other arithmetic  5.49 us (6%)
  local copies, waits for them, and re-layouts  2.8 us (3%)
  Pallas kernels  1.73 us (2%)
    all_to_all x1, starting transfers between devices, on_device(): lax.all_to_all(pieces.reshape(dp, SPARE, LANES), 'dp', 0, 0, axis_index_g...  23.4 us
    all_to_all x1, starting transfers between devices, on_device(): lax.all_to_all(picked.reshape(dp, block_count, LANES), 'dp', 0, 0, axis_i...  13.1 us
    all_to_all x1, starting transfers between devices, on_device(): lax.all_to_all(sums.astype(jnp.bfloat16).reshape(columns, own_slots, rank...  9.72 us
    all_to_all x1, starting transfers between devices, on_device(): lax.all_to_all(jnp.broadcast_to(terms, (LINE,) + terms.shape), 'dp', 0, 0...  8.16 us
    all_to_all x1, starting transfers between devices, on_device(): lax.all_to_all(jnp.broadcast_to(part, (tensor,) + part.shape), 'tensor',...  3.71 us
    all_to_all x1, waiting for transfers between devices, on_device(): lax.all_to_all(pieces.reshape(dp, SPARE, LANES), 'dp', 0, 0, axis_index_g...  3.16 us
    ppermute x1, starting transfers between devices, on_device(): swapped = lax.ppermute(held, 'tensor', far)  3.05 us
    dot_general x1, matrix products, on_device(): lax.dot_general(swapped, swapped_weight, contract_last, preferred_element...  2.49 us
  transfers between devices with their start and end apart: 8, of which 5 were waited for; matrix products, arithmetic and copies ran while one was open for 15% of the time, Pallas kernels for 0%

profile of v6, /device:TPU:2, one launch (start us, length us, event | category | flops | bytes accessed | tf_op | source)
XLA Modules:
  0.0 92.5 jit_solution(10832462614820643760)
XLA Ops:
  0.6 0.0 copy-start
  0.6 0.0 copy-start.2
  0.7 1.7 %shard_map.104 = bf16[384,128]{1,0:T(8,128)(2,1)} custom-call(s32[4]{0:T(128)} %adapter_ref.1, s32[192]{0:T(256)} %owner_ref.1, bf16[2,16,640]{2,1,0:T(8,128)(2,1)} %bitcast.43, bf16[2,16,128]{2,1,0:T(8,128)(2,1)} %up_ref.1), custom_call_target="tpu_custom_call" | custom-call | tf_op jit(solution)/shard_map/pallas_call | solution.py:72
  2.4 23.4 %all-to-all-start = ((bf16[96,4,128]{2,1,0:T(4,128)(2,1)}), bf16[96,4,128]{2,1,0:T(4,128)(2,1)S(1)}, u32[]{:S(2)}, u32[]{:S(2)}) async-start(bf16[96,4,128]{2,1,0:T(4,128)(2,1)} %bitcast.39), calls=%async_computation | async-start | bytes 196608 | tf_op jit(solution)/shard_map/all_to_all | solution.py:120
  25.8 1.9 %collective-permute-start = (bf16[512,128]{1,0:T(8,128)(2,1)}, bf16[512,128]{1,0:T(8,128)(2,1)S(1)}, u32[]{:S(2)}, u32[]{:S(2)}) collective-permute-start(bf16[512,128]{1,0:T(8,128)(2,1)} %param.10), channel_id=1, source_target_pairs={{0,1},{1,0},{2,3},{3,2},{4,5},{5,4},{6,7},{7,6},{8,9},{9,8},{10,11... | collective-permute-start | bytes 393224 | tf_op jit(solution)/shard_map/ppermute | solution.py:113
  27.8 0.7 broadcast_add_fusion
  28.4 0.1 iota_add_fusion
  28.5 0.1 add.69
  28.6 0.7 compare_convert_fusion
  29.3 3.2 %all-to-all-done = bf16[96,4,128]{2,1,0:T(4,128)(2,1)S(1)} async-done(((bf16[96,4,128]{2,1,0:T(4,128)(2,1)}), bf16[96,4,128]{2,1,0:T(4,128)(2,1)S(1)}, u32[]{:S(2)}, u32[]{:S(2)}) %all-to-all-start) | async-done | bytes 98336 | tf_op jit(solution)/shard_map/all_to_all | solution.py:120
  32.5 0.2 fusion.11
  32.6 0.1 reshape.75
  32.8 0.9 convolution_convert_fusion.1
  33.7 13.1 %all-to-all-start.1 = ((bf16[96,4,128]{2,1,0:T(4,128)(2,1)}), bf16[96,4,128]{2,1,0:T(4,128)(2,1)S(1)}, u32[]{:S(2)}, u32[]{:S(2)}) async-start(bf16[96,4,128]{2,1,0:T(4,128)(2,1)} %bitcast.3), calls=%async_computation.1 | async-start | bytes 196608 | tf_op jit(solution)/shard_map/all_to_all | solution.py:135
  46.8 0.0 collective-permute-done
  46.8 1.1 %maximum_select_fusion.1 = bf16[512,256]{1,0:T(8,128)(2,1)S(1)} fusion(bf16[512,128]{1,0:T(8,128)(2,1)S(1)} %collective-permute-done, bf16[512,128]{1,0:T(8,128)(2,1)} %param.10, pred[]{:T(512)S(6)} %eq.38), kind=kLoop, calls=%fused_computation.17 | loop fusion | flops 1179648 | bytes 524289 | tf_op jit(solution)/shard_map/jit(_where)/select_n | solution.py:108
  47.9 2.4 %collective-permute-start.1 = (bf16[512,256]{1,0:T(8,128)(2,1)S(1)}, bf16[512,256]{1,0:T(8,128)(2,1)S(1)}, u32[]{:S(2)}, u32[]{:S(2)}) collective-permute-start(bf16[512,256]{1,0:T(8,128)(2,1)S(1)} %maximum_select_fusion.1), channel_id=1, source_target_pairs={{0,2},{1,3},{2,0},{3,1},{4,6},{5,7},{6,4},{7,5},{8,10},{9,11},{10,... | collective-permute-start | bytes 786440 | tf_op jit(solution)/shard_map/ppermute | solution.py:114
  50.3 0.0 copy-done.2
  50.3 1.1 %broadcast_select_fusion = (bf16[640,512]{1,0:T(8,128)(2,1)}, bf16[640,512]{1,0:T(8,128)(2,1)}) fusion(pred[]{:T(512)S(6)} %lt.19, bf16[640,1024]{1,0:T(8,128)(2,1)S(1)} %copy-done.2), kind=kLoop, calls=%fused_computation.12 | loop fusion | flops 655360 | bytes 2621441 | tf_op jit(solution)/shard_map/jit(_where)/select_n | solution.py:133
  51.5 0.0 copy-start.3
  51.5 1.7 %all-to-all-done.1 = bf16[96,4,128]{2,1,0:T(4,128)(2,1)S(1)} async-done(((bf16[96,4,128]{2,1,0:T(4,128)(2,1)}), bf16[96,4,128]{2,1,0:T(4,128)(2,1)S(1)}, u32[]{:S(2)}, u32[]{:S(2)}) %all-to-all-start.1) | async-done | bytes 98336 | tf_op jit(solution)/shard_map/all_to_all | solution.py:135
  53.2 0.1 copy.48
  53.3 0.1 reshape.70
  53.4 0.0 copy-done
  53.4 0.3 convolution_convert_fusion.3
  53.7 0.0 copy-done.3
  53.8 0.2 convolution_convert_fusion.2
  53.9 0.8 broadcast_in_dim.4
  54.7 3.7 %all-to-all-start.2 = ((bf16[8,4,32,128]{3,2,1,0:T(8,128)(2,1)}), bf16[8,4,32,128]{3,2,1,0:T(8,128)(2,1)S(1)}, u32[]{:S(2)}, u32[]{:S(2)}) async-start(bf16[8,4,32,128]{3,2,1,0:T(8,128)(2,1)} %broadcast_in_dim.4), calls=%async_computation.2 | async-start | bytes 524288 | tf_op jit(solution)/shard_map/all_to_all | solution.py:147
  58.4 0.1 slice_convert_fusion
  58.5 0.1 eq.43
  58.6 0.0 collective-permute-done.1
  58.6 0.9 maximum_select_fusion
  59.5 3.0 %collective-permute-start.2 = (bf16[512,512]{1,0:T(8,128)(2,1)}, bf16[512,512]{1,0:T(8,128)(2,1)}, u32[]{:S(2)}, u32[]{:S(2)}) collective-permute-start(bf16[512,512]{1,0:T(8,128)(2,1)} %maximum_select_fusion), channel_id=1, source_target_pairs={{0,6},{1,7},{2,4},{3,5},{4,2},{5,3},{6,0},{7,1},{8,14},{9,15},{10,... | collective-permute-start | bytes 1572872 | tf_op jit(solution)/shard_map/ppermute | solution.py:115
  62.6 1.8 %all-to-all-done.2 = bf16[8,4,32,128]{3,2,1,0:T(8,128)(2,1)S(1)} async-done(((bf16[8,4,32,128]{3,2,1,0:T(8,128)(2,1)}), bf16[8,4,32,128]{3,2,1,0:T(8,128)(2,1)S(1)}, u32[]{:S(2)}, u32[]{:S(2)}) %all-to-all-start.2) | async-done | bytes 262176 | tf_op jit(solution)/shard_map/all_to_all | solution.py:147
  64.5 0.1 fusion.3
  64.6 0.4 convolution_multiply_fusion.1
  65.0 0.7 broadcast_in_dim.5
  65.7 8.2 %all-to-all-start.3 = ((bf16[8,4,16,128]{3,1,2,0:T(4,128)(2,1)}), bf16[8,4,16,128]{3,1,2,0:T(4,128)(2,1)S(1)}, u32[]{:S(2)}, u32[]{:S(2)}) async-start(bf16[8,4,16,128]{3,1,2,0:T(4,128)(2,1)} %broadcast_in_dim.5), calls=%async_computation.3 | async-start | bytes 262144 | tf_op jit(solution)/shard_map/all_to_all | solution.py:159
  73.9 1.9 %fusion.1 = f32[512,640]{1,0:T(8,128)S(1)} fusion(f32[512,640]{1,0:T(8,128)S(1)} %bitcast.34, bf16[512,512]{1,0:T(8,128)(2,1)} %maximum_select_fusion, bf16[640,512]{1,0:T(8,128)(2,1)} %get-tuple-element.9, f32[512]{0:T(512)S(1)} %get-tuple-element.22), kind=kOutput, calls=%fused_computation.4 | convolution fusion | flops 336199680 | bytes 3803136 | tf_op jit(solution)/shard_map/dot_general | solution.py:180
  75.7 0.0 copy-start.1
  75.7 1.7 %all-to-all-done.3 = bf16[8,4,16,128]{3,1,2,0:T(4,128)(2,1)S(1)} async-done(((bf16[8,4,16,128]{3,1,2,0:T(4,128)(2,1)}), bf16[8,4,16,128]{3,1,2,0:T(4,128)(2,1)S(1)}, u32[]{:S(2)}, u32[]{:S(2)}) %all-to-all-start.3) | async-done | bytes 131104 | tf_op jit(solution)/shard_map/all_to_all | solution.py:159
  77.5 0.2 convolution_convert_fusion
  77.7 0.7 copy.38
  78.4 9.7 %all-to-all-start.4 = ((bf16[12,2,16,128]{3,1,2,0:T(2,128)(2,1)}), bf16[12,2,16,128]{3,1,2,0:T(2,128)(2,1)S(1)}, u32[]{:S(2)}, u32[]{:S(2)}) async-start(bf16[12,2,16,128]{3,1,2,0:T(2,128)(2,1)} %copy.38), calls=%async_computation.4 | async-start | bytes 196608 | tf_op jit(solution)/shard_map/all_to_all | solution.py:171
  88.1 0.0 collective-permute-done.2
  88.1 0.0 copy-done.1
  88.1 2.5 %fusion.2 = bf16[512,640]{1,0:T(8,128)(2,1)} fusion(f32[512,640]{1,0:T(8,128)S(1)} %fusion.1, bf16[512,512]{1,0:T(8,128)(2,1)} %collective-permute-done.2, bf16[640,512]{1,0:T(8,128)(2,1)S(1)} %copy-done.1, f32[512]{0:T(512)S(1)} %get-tuple-element.22), kind=kOutput, calls=%fused_computation.5 | convolution fusion | flops 336527360 | bytes 3147776 | tf_op jit(solution)/shard_map/dot_general | solution.py:182
  90.6 1.2 %all-to-all-done.4 = bf16[12,2,16,128]{3,1,2,0:T(2,128)(2,1)S(1)} async-done(((bf16[12,2,16,128]{3,1,2,0:T(2,128)(2,1)}), bf16[12,2,16,128]{3,1,2,0:T(2,128)(2,1)S(1)}, u32[]{:S(2)}, u32[]{:S(2)}) %all-to-all-start.4) | async-done | bytes 98336 | tf_op jit(solution)/shard_map/all_to_all | solution.py:171
  91.9 0.6 convert_reduce_fusion.1
  (10 shorter events, 0.2 us)
Async XLA Ops:
  0.6 52.8 %copy-start = (bf16[512,640]{1,0:T(8,128)(2,1)S(1)}, bf16[512,640]{1,0:T(8,128)(2,1)}, u32[]{:S(2)}) copy-start(bf16[512,640]{1,0:T(8,128)(2,1)} %param.9) | copy-start | bytes 1966084
  0.6 49.7 %copy-start.2 = (bf16[640,1024]{1,0:T(8,128)(2,1)S(1)}, bf16[640,1024]{1,0:T(8,128)(2,1)}, u32[]{:S(2)}) copy-start(bf16[640,1024]{1,0:T(8,128)(2,1)} %param.11) | copy-start | bytes 3932164
  2.4 30.1 %all-to-all-start = ((bf16[96,4,128]{2,1,0:T(4,128)(2,1)}), bf16[96,4,128]{2,1,0:T(4,128)(2,1)S(1)}, u32[]{:S(2)}, u32[]{:S(2)}) async-start(bf16[96,4,128]{2,1,0:T(4,128)(2,1)} %bitcast.39), calls=%async_computation | async-start | bytes 196608 | tf_op jit(solution)/shard_map/all_to_all | solution.py:120
  25.8 21.0 %collective-permute-start = (bf16[512,128]{1,0:T(8,128)(2,1)}, bf16[512,128]{1,0:T(8,128)(2,1)S(1)}, u32[]{:S(2)}, u32[]{:S(2)}) collective-permute-start(bf16[512,128]{1,0:T(8,128)(2,1)} %param.10), channel_id=1, source_target_pairs={{0,1},{1,0},{2,3},{3,2},{4,5},{5,4},{6,7},{7,6},{8,9},{9,8},{10,11... | collective-permute-start | bytes 393224 | tf_op jit(solution)/shard_map/ppermute | solution.py:113
  33.7 19.5 %all-to-all-start.1 = ((bf16[96,4,128]{2,1,0:T(4,128)(2,1)}), bf16[96,4,128]{2,1,0:T(4,128)(2,1)S(1)}, u32[]{:S(2)}, u32[]{:S(2)}) async-start(bf16[96,4,128]{2,1,0:T(4,128)(2,1)} %bitcast.3), calls=%async_computation.1 | async-start | bytes 196608 | tf_op jit(solution)/shard_map/all_to_all | solution.py:135
  47.9 10.8 %collective-permute-start.1 = (bf16[512,256]{1,0:T(8,128)(2,1)S(1)}, bf16[512,256]{1,0:T(8,128)(2,1)S(1)}, u32[]{:S(2)}, u32[]{:S(2)}) collective-permute-start(bf16[512,256]{1,0:T(8,128)(2,1)S(1)} %maximum_select_fusion.1), channel_id=1, source_target_pairs={{0,2},{1,3},{2,0},{3,1},{4,6},{5,7},{6,4},{7,5},{8,10},{9,11},{10,... | collective-permute-start | bytes 786440 | tf_op jit(solution)/shard_map/ppermute | solution.py:114
  51.5 2.3 %copy-start.3 = (bf16[512,128]{1,0:T(8,128)(2,1)S(1)}, bf16[512,128]{1,0:T(8,128)(2,1)}, u32[]{:S(2)}) copy-start(bf16[512,128]{1,0:T(8,128)(2,1)} %param.10) | copy-start | bytes 393220
  54.7 9.7 %all-to-all-start.2 = ((bf16[8,4,32,128]{3,2,1,0:T(8,128)(2,1)}), bf16[8,4,32,128]{3,2,1,0:T(8,128)(2,1)S(1)}, u32[]{:S(2)}, u32[]{:S(2)}) async-start(bf16[8,4,32,128]{3,2,1,0:T(8,128)(2,1)} %broadcast_in_dim.4), calls=%async_computation.2 | async-start | bytes 524288 | tf_op jit(solution)/shard_map/all_to_all | solution.py:147
  59.5 28.6 %collective-permute-start.2 = (bf16[512,512]{1,0:T(8,128)(2,1)}, bf16[512,512]{1,0:T(8,128)(2,1)}, u32[]{:S(2)}, u32[]{:S(2)}) collective-permute-start(bf16[512,512]{1,0:T(8,128)(2,1)} %maximum_select_fusion), channel_id=1, source_target_pairs={{0,6},{1,7},{2,4},{3,5},{4,2},{5,3},{6,0},{7,1},{8,14},{9,15},{10,... | collective-permute-start | bytes 1572872 | tf_op jit(solution)/shard_map/ppermute | solution.py:115
  65.7 11.7 %all-to-all-start.3 = ((bf16[8,4,16,128]{3,1,2,0:T(4,128)(2,1)}), bf16[8,4,16,128]{3,1,2,0:T(4,128)(2,1)S(1)}, u32[]{:S(2)}, u32[]{:S(2)}) async-start(bf16[8,4,16,128]{3,1,2,0:T(4,128)(2,1)} %broadcast_in_dim.5), calls=%async_computation.3 | async-start | bytes 262144 | tf_op jit(solution)/shard_map/all_to_all | solution.py:159
  75.7 12.4 %copy-start.1 = (bf16[640,512]{1,0:T(8,128)(2,1)S(1)}, bf16[640,512]{1,0:T(8,128)(2,1)}, u32[]{:S(2)}) copy-start(bf16[640,512]{1,0:T(8,128)(2,1)} %get-tuple-element.12) | copy-start | bytes 1966084
  78.4 13.5 %all-to-all-start.4 = ((bf16[12,2,16,128]{3,1,2,0:T(2,128)(2,1)}), bf16[12,2,16,128]{3,1,2,0:T(2,128)(2,1)S(1)}, u32[]{:S(2)}, u32[]{:S(2)}) async-start(bf16[12,2,16,128]{3,1,2,0:T(2,128)(2,1)} %copy.38), calls=%async_computation.4 | async-start | bytes 196608 | tf_op jit(solution)/shard_map/all_to_all | solution.py:171

commit v7 on v6

--- a/solution.py
+++ b/solution.py
@@ -11,7 +11,7 @@
 LINE = 8
 FIRST_Z = 9
 FIRST_Y = 4
-LAST_Z = 7
+LAST_Z = 6
 FIRST_X = 2
 LANES = 128
 CORES = 2

time: 93.4 us -> 94 us (level)
  the two profiles are of different devices: /device:TPU:2 before, /device:TPU:4 now
where the time goes in v7:
time: 94 us; the launch traced here: 93.3 us
  starting transfers between devices  66.3 us (71%)
  waiting for transfers between devices  9.59 us (10%)
  matrix products  6.46 us (7%)
  other arithmetic  5.49 us (6%)
  local copies, waits for them, and re-layouts  2.8 us (3%)
  Pallas kernels  1.73 us (2%)
    all_to_all x1, starting transfers between devices, on_device(): lax.all_to_all(pieces.reshape(dp, SPARE, LANES), 'dp', 0, 0, axis_index_g...  23.4 us
    all_to_all x1, starting transfers between devices, on_device(): lax.all_to_all(picked.reshape(dp, block_count, LANES), 'dp', 0, 0, axis_i...  13.1 us
    all_to_all x1, starting transfers between devices, on_device(): lax.all_to_all(sums.astype(jnp.bfloat16).reshape(columns, own_slots, rank...  10.5 us
    all_to_all x1, starting transfers between devices, on_device(): lax.all_to_all(jnp.broadcast_to(terms, (LINE,) + terms.shape), 'dp', 0, 0...  8.16 us
    all_to_all x1, starting transfers between devices, on_device(): lax.all_to_all(jnp.broadcast_to(part, (tensor,) + part.shape), 'tensor',...  3.36 us
    all_to_all x1, waiting for transfers between devices, on_device(): lax.all_to_all(pieces.reshape(dp, SPARE, LANES), 'dp', 0, 0, axis_index_g...  3.16 us
    ppermute x1, starting transfers between devices, on_device(): held = both(held, lax.ppermute(held, 'tensor', pair), my_x % 2 == 0)  3.1 us
    ppermute x1, starting transfers between devices, on_device(): swapped = lax.ppermute(held, 'tensor', far)  2.77 us
  transfers between devices with their start and end apart: 8, of which 5 were waited for; matrix products, arithmetic and copies ran while one was open for 15% of the time, Pallas kernels for 0%

profile of v7, /device:TPU:4, one launch (start us, length us, event | category | flops | bytes accessed | tf_op | source)
XLA Modules:
  0.0 93.3 jit_solution(16946918360620208775)
XLA Ops:
  0.6 0.0 copy-start
  0.6 0.0 copy-start.2
  0.7 1.7 %shard_map.104 = bf16[384,128]{1,0:T(8,128)(2,1)} custom-call(s32[4]{0:T(128)} %adapter_ref.1, s32[192]{0:T(256)} %owner_ref.1, bf16[2,16,640]{2,1,0:T(8,128)(2,1)} %bitcast.43, bf16[2,16,128]{2,1,0:T(8,128)(2,1)} %up_ref.1), custom_call_target="tpu_custom_call" | custom-call | tf_op jit(solution)/shard_map/pallas_call | solution.py:72
  2.4 23.4 %all-to-all-start = ((bf16[96,4,128]{2,1,0:T(4,128)(2,1)}), bf16[96,4,128]{2,1,0:T(4,128)(2,1)S(1)}, u32[]{:S(2)}, u32[]{:S(2)}) async-start(bf16[96,4,128]{2,1,0:T(4,128)(2,1)} %bitcast.39), calls=%async_computation | async-start | bytes 196608 | tf_op jit(solution)/shard_map/all_to_all | solution.py:120
  25.8 1.9 %collective-permute-start = (bf16[512,128]{1,0:T(8,128)(2,1)}, bf16[512,128]{1,0:T(8,128)(2,1)S(1)}, u32[]{:S(2)}, u32[]{:S(2)}) collective-permute-start(bf16[512,128]{1,0:T(8,128)(2,1)} %param.10), channel_id=1, source_target_pairs={{0,1},{1,0},{2,3},{3,2},{4,5},{5,4},{6,7},{7,6},{8,9},{9,8},{10,11... | collective-permute-start | bytes 393224 | tf_op jit(solution)/shard_map/ppermute | solution.py:113
  27.8 0.7 broadcast_add_fusion
  28.4 0.1 iota_add_fusion
  28.5 0.1 add.69
  28.6 0.7 compare_convert_fusion
  29.3 3.2 %all-to-all-done = bf16[96,4,128]{2,1,0:T(4,128)(2,1)S(1)} async-done(((bf16[96,4,128]{2,1,0:T(4,128)(2,1)}), bf16[96,4,128]{2,1,0:T(4,128)(2,1)S(1)}, u32[]{:S(2)}, u32[]{:S(2)}) %all-to-all-start) | async-done | bytes 98336 | tf_op jit(solution)/shard_map/all_to_all | solution.py:120
  32.5 0.2 fusion.11
  32.6 0.1 reshape.75
  32.8 0.9 convolution_convert_fusion.1
  33.7 13.1 %all-to-all-start.1 = ((bf16[96,4,128]{2,1,0:T(4,128)(2,1)}), bf16[96,4,128]{2,1,0:T(4,128)(2,1)S(1)}, u32[]{:S(2)}, u32[]{:S(2)}) async-start(bf16[96,4,128]{2,1,0:T(4,128)(2,1)} %bitcast.3), calls=%async_computation.1 | async-start | bytes 196608 | tf_op jit(solution)/shard_map/all_to_all | solution.py:135
  46.8 0.0 collective-permute-done
  46.8 1.1 %maximum_select_fusion.1 = bf16[512,256]{1,0:T(8,128)(2,1)S(1)} fusion(bf16[512,128]{1,0:T(8,128)(2,1)S(1)} %collective-permute-done, bf16[512,128]{1,0:T(8,128)(2,1)} %param.10, pred[]{:T(512)S(6)} %eq.38), kind=kLoop, calls=%fused_computation.17 | loop fusion | flops 1179648 | bytes 524289 | tf_op jit(solution)/shard_map/jit(_where)/select_n | solution.py:108
  47.9 3.1 %collective-permute-start.1 = (bf16[512,256]{1,0:T(8,128)(2,1)S(1)}, bf16[512,256]{1,0:T(8,128)(2,1)S(1)}, u32[]{:S(2)}, u32[]{:S(2)}) collective-permute-start(bf16[512,256]{1,0:T(8,128)(2,1)S(1)} %maximum_select_fusion.1), channel_id=1, source_target_pairs={{0,2},{1,3},{2,0},{3,1},{4,6},{5,7},{6,4},{7,5},{8,10},{9,11},{10,... | collective-permute-start | bytes 786440 | tf_op jit(solution)/shard_map/ppermute | solution.py:114
  51.0 0.0 copy-done.2
  51.0 1.1 %broadcast_select_fusion = (bf16[640,512]{1,0:T(8,128)(2,1)}, bf16[640,512]{1,0:T(8,128)(2,1)}) fusion(pred[]{:T(512)S(6)} %lt.19, bf16[640,1024]{1,0:T(8,128)(2,1)S(1)} %copy-done.2), kind=kLoop, calls=%fused_computation.12 | loop fusion | flops 655360 | bytes 2621441 | tf_op jit(solution)/shard_map/jit(_where)/select_n | solution.py:133
  52.1 0.0 copy-start.3
  52.1 1.0 %all-to-all-done.1 = bf16[96,4,128]{2,1,0:T(4,128)(2,1)S(1)} async-done(((bf16[96,4,128]{2,1,0:T(4,128)(2,1)}), bf16[96,4,128]{2,1,0:T(4,128)(2,1)S(1)}, u32[]{:S(2)}, u32[]{:S(2)}) %all-to-all-start.1) | async-done | bytes 98336 | tf_op jit(solution)/shard_map/all_to_all | solution.py:135
  53.2 0.1 copy.48
  53.3 0.1 reshape.70
  53.4 0.0 copy-done
  53.4 0.3 convolution_convert_fusion.3
  53.7 0.0 copy-done.3
  53.7 0.2 convolution_convert_fusion.2
  53.9 0.8 broadcast_in_dim.4
  54.7 3.4 %all-to-all-start.2 = ((bf16[8,4,32,128]{3,2,1,0:T(8,128)(2,1)}), bf16[8,4,32,128]{3,2,1,0:T(8,128)(2,1)S(1)}, u32[]{:S(2)}, u32[]{:S(2)}) async-start(bf16[8,4,32,128]{3,2,1,0:T(8,128)(2,1)} %broadcast_in_dim.4), calls=%async_computation.2 | async-start | bytes 524288 | tf_op jit(solution)/shard_map/all_to_all | solution.py:147
  58.1 0.1 slice_convert_fusion
  58.2 0.1 eq.43
  58.3 0.0 collective-permute-done.1
  58.3 0.9 maximum_select_fusion
  59.2 2.8 %collective-permute-start.2 = (bf16[512,512]{1,0:T(8,128)(2,1)}, bf16[512,512]{1,0:T(8,128)(2,1)}, u32[]{:S(2)}, u32[]{:S(2)}) collective-permute-start(bf16[512,512]{1,0:T(8,128)(2,1)} %maximum_select_fusion), channel_id=1, source_target_pairs={{0,6},{1,7},{2,4},{3,5},{4,2},{5,3},{6,0},{7,1},{8,14},{9,15},{10,... | collective-permute-start | bytes 1572872 | tf_op jit(solution)/shard_map/ppermute | solution.py:115
  62.0 1.6 %all-to-all-done.2 = bf16[8,4,32,128]{3,2,1,0:T(8,128)(2,1)S(1)} async-done(((bf16[8,4,32,128]{3,2,1,0:T(8,128)(2,1)}), bf16[8,4,32,128]{3,2,1,0:T(8,128)(2,1)S(1)}, u32[]{:S(2)}, u32[]{:S(2)}) %all-to-all-start.2) | async-done | bytes 262176 | tf_op jit(solution)/shard_map/all_to_all | solution.py:147
  63.6 0.1 fusion.3
  63.7 0.4 convolution_multiply_fusion.1
  64.2 0.7 broadcast_in_dim.5
  64.8 8.2 %all-to-all-start.3 = ((bf16[8,4,16,128]{3,1,2,0:T(4,128)(2,1)}), bf16[8,4,16,128]{3,1,2,0:T(4,128)(2,1)S(1)}, u32[]{:S(2)}, u32[]{:S(2)}) async-start(bf16[8,4,16,128]{3,1,2,0:T(4,128)(2,1)} %broadcast_in_dim.5), calls=%async_computation.3 | async-start | bytes 262144 | tf_op jit(solution)/shard_map/all_to_all | solution.py:159
  73.0 1.9 %fusion.1 = f32[512,640]{1,0:T(8,128)S(1)} fusion(f32[512,640]{1,0:T(8,128)S(1)} %bitcast.34, bf16[512,512]{1,0:T(8,128)(2,1)} %maximum_select_fusion, bf16[640,512]{1,0:T(8,128)(2,1)} %get-tuple-element.9, f32[512]{0:T(512)S(1)} %get-tuple-element.22), kind=kOutput, calls=%fused_computation.4 | convolution fusion | flops 336199680 | bytes 3803136 | tf_op jit(solution)/shard_map/dot_general | solution.py:180
  74.9 0.0 copy-start.1
  74.9 2.5 %all-to-all-done.3 = bf16[8,4,16,128]{3,1,2,0:T(4,128)(2,1)S(1)} async-done(((bf16[8,4,16,128]{3,1,2,0:T(4,128)(2,1)}), bf16[8,4,16,128]{3,1,2,0:T(4,128)(2,1)S(1)}, u32[]{:S(2)}, u32[]{:S(2)}) %all-to-all-start.3) | async-done | bytes 131104 | tf_op jit(solution)/shard_map/all_to_all | solution.py:159
  77.5 0.2 convolution_convert_fusion
  77.7 0.7 copy.38
  78.4 10.5 %all-to-all-start.4 = ((bf16[12,2,16,128]{3,1,2,0:T(2,128)(2,1)}), bf16[12,2,16,128]{3,1,2,0:T(2,128)(2,1)S(1)}, u32[]{:S(2)}, u32[]{:S(2)}) async-start(bf16[12,2,16,128]{3,1,2,0:T(2,128)(2,1)} %copy.38), calls=%async_computation.4 | async-start | bytes 196608 | tf_op jit(solution)/shard_map/all_to_all | solution.py:171
  88.9 0.0 collective-permute-done.2
  88.9 0.0 copy-done.1
  88.9 2.5 %fusion.2 = bf16[512,640]{1,0:T(8,128)(2,1)} fusion(f32[512,640]{1,0:T(8,128)S(1)} %fusion.1, bf16[512,512]{1,0:T(8,128)(2,1)} %collective-permute-done.2, bf16[640,512]{1,0:T(8,128)(2,1)S(1)} %copy-done.1, f32[512]{0:T(512)S(1)} %get-tuple-element.22), kind=kOutput, calls=%fused_computation.5 | convolution fusion | flops 336527360 | bytes 3147776 | tf_op jit(solution)/shard_map/dot_general | solution.py:182
  91.4 1.3 %all-to-all-done.4 = bf16[12,2,16,128]{3,1,2,0:T(2,128)(2,1)S(1)} async-done(((bf16[12,2,16,128]{3,1,2,0:T(2,128)(2,1)}), bf16[12,2,16,128]{3,1,2,0:T(2,128)(2,1)S(1)}, u32[]{:S(2)}, u32[]{:S(2)}) %all-to-all-start.4) | async-done | bytes 98336 | tf_op jit(solution)/shard_map/all_to_all | solution.py:171
  92.7 0.6 convert_reduce_fusion.1
  (10 shorter events, 0.2 us)
Async XLA Ops:
  0.6 52.8 %copy-start = (bf16[512,640]{1,0:T(8,128)(2,1)S(1)}, bf16[512,640]{1,0:T(8,128)(2,1)}, u32[]{:S(2)}) copy-start(bf16[512,640]{1,0:T(8,128)(2,1)} %param.9) | copy-start | bytes 1966084
  0.6 50.3 %copy-start.2 = (bf16[640,1024]{1,0:T(8,128)(2,1)S(1)}, bf16[640,1024]{1,0:T(8,128)(2,1)}, u32[]{:S(2)}) copy-start(bf16[640,1024]{1,0:T(8,128)(2,1)} %param.11) | copy-start | bytes 3932164
  2.4 30.1 %all-to-all-start = ((bf16[96,4,128]{2,1,0:T(4,128)(2,1)}), bf16[96,4,128]{2,1,0:T(4,128)(2,1)S(1)}, u32[]{:S(2)}, u32[]{:S(2)}) async-start(bf16[96,4,128]{2,1,0:T(4,128)(2,1)} %bitcast.39), calls=%async_computation | async-start | bytes 196608 | tf_op jit(solution)/shard_map/all_to_all | solution.py:120
  25.8 21.0 %collective-permute-start = (bf16[512,128]{1,0:T(8,128)(2,1)}, bf16[512,128]{1,0:T(8,128)(2,1)S(1)}, u32[]{:S(2)}, u32[]{:S(2)}) collective-permute-start(bf16[512,128]{1,0:T(8,128)(2,1)} %param.10), channel_id=1, source_target_pairs={{0,1},{1,0},{2,3},{3,2},{4,5},{5,4},{6,7},{7,6},{8,9},{9,8},{10,11... | collective-permute-start | bytes 393224 | tf_op jit(solution)/shard_map/ppermute | solution.py:113
  33.7 19.5 %all-to-all-start.1 = ((bf16[96,4,128]{2,1,0:T(4,128)(2,1)}), bf16[96,4,128]{2,1,0:T(4,128)(2,1)S(1)}, u32[]{:S(2)}, u32[]{:S(2)}) async-start(bf16[96,4,128]{2,1,0:T(4,128)(2,1)} %bitcast.3), calls=%async_computation.1 | async-start | bytes 196608 | tf_op jit(solution)/shard_map/all_to_all | solution.py:135
  47.9 10.4 %collective-permute-start.1 = (bf16[512,256]{1,0:T(8,128)(2,1)S(1)}, bf16[512,256]{1,0:T(8,128)(2,1)S(1)}, u32[]{:S(2)}, u32[]{:S(2)}) collective-permute-start(bf16[512,256]{1,0:T(8,128)(2,1)S(1)} %maximum_select_fusion.1), channel_id=1, source_target_pairs={{0,2},{1,3},{2,0},{3,1},{4,6},{5,7},{6,4},{7,5},{8,10},{9,11},{10,... | collective-permute-start | bytes 786440 | tf_op jit(solution)/shard_map/ppermute | solution.py:114
  52.1 1.6 %copy-start.3 = (bf16[512,128]{1,0:T(8,128)(2,1)S(1)}, bf16[512,128]{1,0:T(8,128)(2,1)}, u32[]{:S(2)}) copy-start(bf16[512,128]{1,0:T(8,128)(2,1)} %param.10) | copy-start | bytes 393220
  54.7 8.8 %all-to-all-start.2 = ((bf16[8,4,32,128]{3,2,1,0:T(8,128)(2,1)}), bf16[8,4,32,128]{3,2,1,0:T(8,128)(2,1)S(1)}, u32[]{:S(2)}, u32[]{:S(2)}) async-start(bf16[8,4,32,128]{3,2,1,0:T(8,128)(2,1)} %broadcast_in_dim.4), calls=%async_computation.2 | async-start | bytes 524288 | tf_op jit(solution)/shard_map/all_to_all | solution.py:147
  59.2 29.7 %collective-permute-start.2 = (bf16[512,512]{1,0:T(8,128)(2,1)}, bf16[512,512]{1,0:T(8,128)(2,1)}, u32[]{:S(2)}, u32[]{:S(2)}) collective-permute-start(bf16[512,512]{1,0:T(8,128)(2,1)} %maximum_select_fusion), channel_id=1, source_target_pairs={{0,6},{1,7},{2,4},{3,5},{4,2},{5,3},{6,0},{7,1},{8,14},{9,15},{10,... | collective-permute-start | bytes 1572872 | tf_op jit(solution)/shard_map/ppermute | solution.py:115
  64.8 12.6 %all-to-all-start.3 = ((bf16[8,4,16,128]{3,1,2,0:T(4,128)(2,1)}), bf16[8,4,16,128]{3,1,2,0:T(4,128)(2,1)S(1)}, u32[]{:S(2)}, u32[]{:S(2)}) async-start(bf16[8,4,16,128]{3,1,2,0:T(4,128)(2,1)} %broadcast_in_dim.5), calls=%async_computation.3 | async-start | bytes 262144 | tf_op jit(solution)/shard_map/all_to_all | solution.py:159
  74.9 14.0 %copy-start.1 = (bf16[640,512]{1,0:T(8,128)(2,1)S(1)}, bf16[640,512]{1,0:T(8,128)(2,1)}, u32[]{:S(2)}) copy-start(bf16[640,512]{1,0:T(8,128)(2,1)} %get-tuple-element.12) | copy-start | bytes 1966084
  78.4 14.3 %all-to-all-start.4 = ((bf16[12,2,16,128]{3,1,2,0:T(2,128)(2,1)}), bf16[12,2,16,128]{3,1,2,0:T(2,128)(2,1)S(1)}, u32[]{:S(2)}, u32[]{:S(2)}) async-start(bf16[12,2,16,128]{3,1,2,0:T(2,128)(2,1)} %copy.38), calls=%async_computation.4 | async-start | bytes 196608 | tf_op jit(solution)/shard_map/all_to_all | solution.py:171
